TPU v7x, 32 devices: a whole 2x2x4 slice. The times are simulated.
32 devices in a mesh: groups: 2 (over x), gx: 16 (over z, y, core).
Axes of the slice: x: 2, y: 2, z: 4, core: 2. Of those that a mesh axis runs over, the one named last changes fastest.
Arguments:
- features: bfloat16 [32, 256, 16, 128], P(None, ('groups', 'gx')), parts along dimension 1, may hold values from -6 to 6
- active_blocks: int32 [32, 2, 16], P(('groups', 'gx')), parts along dimension 0, may hold values 0 or 1
- weight_fine: bfloat16 [32, 32, 3, 3, 3], replicated, may hold values from -0.21875 to 0.21875
- weight_coarse: bfloat16 [64, 32, 3, 3, 3], replicated, may hold values from -0.21875 to 0.21875
- weight_up: bfloat16 [32, 64], replicated, may hold values from -0.75 to 0.75
- cotangent: bfloat16 [32, 256, 16, 128], P(None, ('groups', 'gx')), parts along dimension 1, may hold values from -6 to 6
Outputs:
- net_output: bfloat16 [32, 256, 16, 128], P(None, ('groups', 'gx')), parts along dimension 1
- grad_features: float32 [32, 256, 16, 128], P(None, ('groups', 'gx')), parts along dimension 1
- grad_fine: float32 [64, 32, 3, 3, 3], P('groups'), parts along dimension 0
- grad_coarse: float32 [128, 32, 3, 3, 3], P('groups'), parts along dimension 0
- grad_up: float32 [64, 64], P('groups'), parts along dimension 0
There are 2 independent parts, one for each index of `groups`. A program takes and returns all parts, laid end to end along the dimension named above; an argument that names none is the same for every part. Nothing has to cross between parts.
All inputs are finite; a program needn't handle non-finite values. No bound on the sum of `active_blocks` on one device may be relied on, other than what follows from the above.
Results may differ from a plain program's by a relative error of at most 0.01.
Values may be sent and summed in bfloat16 or wider, within the bound.
A program may use at most 128 MiB of HBM per device.

v0:
```python
import math

import jax
import jax.numpy as jnp
from jax import lax
from jax.sharding import PartitionSpec as P


def extended(block, sides, width):
    for axis, dim in sides:
        count = lax.axis_size(axis)
        forward = [(i, i + 1) for i in range(count - 1)]
        backward = [(target, source) for source, target in forward]
        low = lax.ppermute(
            lax.slice_in_dim(block, block.shape[dim] - width, None, axis=dim), axis, forward
        )
        high = lax.ppermute(lax.slice_in_dim(block, 0, width, axis=dim), axis, backward)
        block = jnp.concatenate([low, block, high], axis=dim)
    return block


def conv_rows(padded, weight):
    chans = padded.shape[0]
    extent_x = padded.shape[1] - 2
    extent_z, extent_y = (padded.shape[2], padded.shape[3])
    widened = jnp.pad(padded, ((0, 0), (0, 0), (1, 1), (1, 1)))
    total = jnp.zeros((weight.shape[0], extent_x, extent_z, extent_y), jnp.float32)
    for i in range(3):
        slab = widened[:, i : i + extent_x]
        stacked = jnp.concatenate(
            [slab[:, :, j : j + extent_z, k : k + extent_y] for j in range(3) for k in range(3)],
            axis=0,
        )
        taps = weight[:, :, i].transpose(0, 2, 3, 1).reshape(weight.shape[0], 9 * chans)
        total = total + jnp.einsum(
            "oc,cxzy->oxzy", taps, stacked, preferred_element_type=jnp.float32
        )
    return total


def flip_weight(weight):
    return jnp.flip(weight, (2, 3, 4)).transpose(1, 0, 2, 3, 4)


def conv_back_owned(widened, weight):
    return conv_rows(widened, flip_weight(weight))


def weight_grad(padded, grad):
    widened = jnp.pad(padded, ((0, 0), (0, 0), (1, 1), (1, 1)))
    extent_x, extent_z, extent_y = (grad.shape[1], grad.shape[2], grad.shape[3])
    tap_list = []
    for i in range(3):
        for j in range(3):
            for k in range(3):
                window = widened[:, i : i + extent_x, j : j + extent_z, k : k + extent_y]
                tap_list.append(
                    jnp.einsum("oxzy,cxzy->oc", grad, window, preferred_element_type=jnp.float32)
                )
    stacked = jnp.stack(tap_list, axis=2)
    return stacked.reshape(stacked.shape[0], stacked.shape[1], 3, 3, 3)


def expand_mask(blocks, factor):
    values = blocks.astype(jnp.float32)
    size_x, size_z, size_y = values.shape
    values = jnp.broadcast_to(
        values[:, None, :, None, :, None], (size_x, factor, size_z, factor, size_y, factor)
    )
    return values.reshape(size_x * factor, size_z * factor, size_y * factor)


def pool_sum(values):
    chans, size_x, size_z, size_y = values.shape
    return values.reshape(chans, size_x // 2, 2, size_z // 2, 2, size_y // 2, 2).sum(axis=(2, 4, 6))


def spread(values):
    chans, size_x, size_z, size_y = values.shape
    wide_view = jnp.broadcast_to(
        values[:, :, None, :, None, :, None], (chans, size_x, 2, size_z, 2, size_y, 2)
    )
    return wide_view.reshape(chans, size_x * 2, size_z * 2, size_y * 2)


def silu_slope(values):
    sigma = jax.nn.sigmoid(values)
    return sigma * (1.0 + values * (1.0 - sigma))


def per_device(features, active_blocks, weight_fine, weight_coarse, weight_up, cotangent):
    cell_count = features.shape[1] * lax.axis_size("gx") * features.shape[2] * features.shape[3]
    factor = 1.0 / math.sqrt(cell_count)
    fine_mask = expand_mask(active_blocks, 8)
    coarse_mask = expand_mask(active_blocks, 4)
    padded = extended(features, (("gx", 1),), 1)
    pre_fine = conv_rows(padded, weight_fine)
    hidden_fine = (jax.nn.silu(pre_fine) * fine_mask).astype(jnp.bfloat16)
    pooled = (pool_sum(hidden_fine.astype(jnp.float32)) * 0.125).astype(jnp.bfloat16)
    pooled_pad = extended(pooled, (("gx", 1),), 1)
    pre_coarse = conv_rows(pooled_pad, weight_coarse)
    hidden_coarse = (jax.nn.silu(pre_coarse) * coarse_mask).astype(jnp.bfloat16)
    lifted = jnp.einsum(
        "oc,cxzy->oxzy", weight_up, hidden_coarse, preferred_element_type=jnp.float32
    )
    net_output = (hidden_fine.astype(jnp.float32) + fine_mask * spread(lifted)).astype(jnp.bfloat16)
    grad_lift = pool_sum(cotangent.astype(jnp.float32) * fine_mask)
    grad_up = factor * jnp.einsum(
        "oxzy,cxzy->oc",
        grad_lift,
        hidden_coarse.astype(jnp.float32),
        precision=lax.Precision.HIGHEST,
    )
    grad_hidden_coarse = jnp.einsum(
        "oc,oxzy->cxzy", weight_up.astype(jnp.float32), grad_lift, precision=lax.Precision.HIGHEST
    )
    grad_pre_coarse = (grad_hidden_coarse * coarse_mask * silu_slope(pre_coarse)).astype(
        jnp.bfloat16
    )
    grad_coarse = factor * weight_grad(pooled_pad, grad_pre_coarse)
    coarse_wide = extended(grad_pre_coarse, (("gx", 1),), 1)
    grad_pooled = conv_back_owned(coarse_wide, weight_coarse)
    grad_hidden = cotangent.astype(jnp.float32) + spread(grad_pooled) * 0.125
    grad_pre_fine = (grad_hidden * fine_mask * silu_slope(pre_fine)).astype(jnp.bfloat16)
    grad_fine = factor * weight_grad(padded, grad_pre_fine)
    fine_wide = extended(grad_pre_fine, (("gx", 1),), 1)
    grad_features = conv_back_owned(fine_wide, weight_fine)
    grad_fine, grad_coarse, grad_up = lax.psum((grad_fine, grad_coarse, grad_up), "gx")
    return (net_output, grad_features, grad_fine, grad_coarse, grad_up)


def solution(mesh):
    return jax.shard_map(
        per_device,
        mesh=mesh,
        in_specs=(
            P(None, ("groups", "gx"), None, None),
            P(("groups", "gx"), None, None),
            P(),
            P(),
            P(),
            P(None, ("groups", "gx"), None, None),
        ),
        out_specs=(
            P(None, ("groups", "gx"), None, None),
            P(None, ("groups", "gx"), None, None),
            P("groups", None, None, None, None),
            P("groups", None, None, None, None),
            P("groups", None),
        ),
        check_vma=False,
    )
```

profile of v0, /device:TPU:0, one launch (start us, length us, event | category | flops | bytes accessed | tf_op | source)
XLA Modules:
  0.0 392.2 jit_solution(4430253358574457202)
XLA Ops:
  34.8 4.8 %convert_multiply_fusion = (f32[32,8,16,128]{3,0,2,1:T(8,128)}, f32[32,8,16,128]{3,0,2,1:T(8,128)}, f32[8,16,128,32]{2,3,1,0:T(8,128)}) fusion(f32[16,128]{1,0:T(8,128)S(1)} %broadcast_in_dim.32, bf16[32,8,16,128]{3,2,1,0:T(8,128)(2,1)S(1)} %copy-done.11, bf16[288,8,16,128]{3,0,2,1:T(8,128)(2,1)S(1)} %get-tuple-element.46, ...), kind=kOutput, calls=%fused_computation.21 | convolution fusion | flops 307757056 | bytes 20998144 | tf_op jit(solution)/shard_map/oc,cxzy->oxzy/dot_general | solution.py:35
  39.7 6.3 %copy.182 = f32[32,8,16,128]{0,3,2,1:T(8,128)} copy(f32[32,8,16,128]{3,0,2,1:T(8,128)} %get-tuple-element.150) | data formatting | bytes 4194304 | tf_op jit(solution)/shard_map/convert_element_type | solution.py:106
  46.0 8.8 %reduce_sum.18 = f32[32,4,8,64]{0,3,2,1:T(8,128)S(1)} reduce(f32[32,4,2,8,2,64,2]{0,6,5,4,3,2,1:T(2,128)} %bitcast.669, f32[]{:T(128)} %constant.7.clone.1), dimensions={2,4,6}, to_apply=%region_0.1 | reduce | flops 458752 | bytes 2359300 | tf_op jit(solution)/shard_map/reduce_sum | solution.py:75
  54.9 5.5 %collective-permute-start.2 = (bf16[32,1,8,64]{0,3,2,1:T(8,128)(2,1)S(1)}, bf16[32,1,8,64]{0,3,2,1:T(8,128)(2,1)S(1)}, u32[]{:S(2)}, u32[]{:S(2)}) collective-permute-start(bf16[32,1,8,64]{0,3,2,1:T(8,128)(2,1)S(1)} %get-tuple-element.135), channel_id=1, source_target_pairs={{0,1},{1,2},{2,3},{3,4},{4,5},{5,6},{6,7},{7,8},{8,9},{9,10},{10,1... | collective-permute-start | bytes 98312 | tf_op jit(solution)/shard_map/ppermute | solution.py:14
  64.2 6.7 %copy.190 = f32[32,8,16,128]{0,3,2,1:T(8,128)} copy(f32[32,8,16,128]{3,0,2,1:T(8,128)} %get-tuple-element.149) | data formatting | bytes 4194304 | tf_op jit(solution)/shard_map/mul | solution.py:107
  70.9 9.7 %reduce_sum.19 = f32[32,4,8,64]{0,3,2,1:T(8,128)} reduce(f32[32,4,2,8,2,64,2]{0,6,5,4,3,2,1:T(2,128)} %bitcast.668, f32[]{:T(128)} %constant.7.clone.1), dimensions={2,4,6}, to_apply=%region_1.2 | reduce | flops 458752 | bytes 2359300 | tf_op jit(solution)/shard_map/reduce_sum | solution.py:75
  82.6 4.2 %fusion.159 = (bf16[32,4,8,64]{0,3,2,1:T(8,128)(2,1)}, bf16[32,4,8,64]{0,3,2,1:T(8,128)(2,1)}, bf16[32,4,8,64]{0,3,2,1:T(8,128)(2,1)}, bf16[32,4,8,64]{0,3,2,1:T...) fusion(bf16[32,6,10,66]{0,3,2,1:T(8,128)(2,1)S(1)} %select_maxi, ...), kind=kLoop, calls=%fused_computation.318 | loop fusion | bytes 4980736 | tf_op jit(solution)/shard_map/slice | solution.py:31
  88.8 6.6 %concatenate.87 = bf16[288,4,8,64]{0,3,2,1:T(8,128)(2,1)} concatenate(bf16[32,4,8,64]{0,3,2,1:T(8,128)(2,1)} %get-tuple-element.103, bf16[32,4,8,64]{0,3,2,1:T(8,128)(2,1)} %get-tuple-element.102, bf16[32,4,8,64]{0,3,2,1:T(8,128)(2,1)} %get-tuple-element.101, bf16[32,4,8,64]{0,3,2,1:T(8,128)(2,1)} %get-tuple-element.100, bf16[32,4,8,64]{0,3,2,1:T(8,128)(2,1)S(1)} %get-tuple-element.134, ...), dimensions={0} | concatenate | bytes 2359296 | tf_op jit(solution)/shard_map/concatenate | solution.py:30
  98.4 6.5 %concatenate.85 = bf16[288,4,8,64]{0,3,2,1:T(8,128)(2,1)} concatenate(bf16[32,4,8,64]{0,3,2,1:T(8,128)(2,1)} %get-tuple-element.111, bf16[32,4,8,64]{0,3,2,1:T(8,128)(2,1)} %get-tuple-element.110, bf16[32,4,8,64]{0,3,2,1:T(8,128)(2,1)} %get-tuple-element.109, bf16[32,4,8,64]{0,3,2,1:T(8,128)(2,1)} %get-tuple-element.108, bf16[32,4,8,64]{0,3,2,1:T(8,128)(2,1)S(1)} %multiply_convert_fusion.1, ...), dimensions={0} | concatenate | bytes 2359296 | tf_op jit(solution)/shard_map/concatenate | solution.py:30
  107.9 6.6 %concatenate.84 = bf16[288,4,8,64]{0,3,2,1:T(8,128)(2,1)} concatenate(bf16[32,4,8,64]{0,3,2,1:T(8,128)(2,1)} %get-tuple-element.118, bf16[32,4,8,64]{0,3,2,1:T(8,128)(2,1)} %get-tuple-element.117, bf16[32,4,8,64]{0,3,2,1:T(8,128)(2,1)} %get-tuple-element.116, bf16[32,4,8,64]{0,3,2,1:T(8,128)(2,1)} %get-tuple-element.115, bf16[32,4,8,64]{0,3,2,1:T(8,128)(2,1)S(1)} %copy-done.6, ...), dimensions={0} | concatenate | bytes 2359296 | tf_op jit(solution)/shard_map/concatenate | solution.py:30
  135.9 7.5 %broadcast_in_dim.35 = f32[32,4,2,8,2,64,2]{0,6,5,4,3,2,1:T(2,128)} broadcast(f32[32,4,8,64]{0,3,2,1:T(8,128)S(1)} %copy.187), dimensions={0,1,3,5} | broadcast | bytes 2359296 | tf_op jit(solution)/shard_map/broadcast_in_dim | solution.py:80
  143.4 6.3 %copy.188 = f32[32,8,16,128]{3,0,2,1:T(8,128)} copy(f32[32,8,16,128]{0,3,2,1:T(8,128)} %bitcast.670) | data formatting | bytes 4194304 | tf_op jit(solution)/shard_map/reshape | solution.py:83
  149.7 63.2 %psum.23 = f32[32,64]{1,0:T(8,128)} all-reduce(f32[32,64]{1,0:T(8,128)S(1)} %copy-done.31), channel_id=1, replica_groups=mesh['groups'=2,'gx'=16] {'gx'}, use_global_device_ids=true, to_apply=%region_4.5 | all-reduce | flops 2048 | bytes 16384 | tf_op jit(solution)/shard_map/psum | solution.py:128
  214.6 4.1 %fusion.157 = (bf16[64,4,8,64]{0,3,2,1:T(8,128)(2,1)}, bf16[64,4,8,64]{0,3,2,1:T(8,128)(2,1)}, bf16[64,4,8,64]{0,3,2,1:T(8,128)(2,1)}, bf16[64,4,8,64]{0,3,2,1:T...) fusion(bf16[64,6,10,66]{0,3,2,1:T(8,128)(2,1)S(1)} %select_maxi, ...), kind=kLoop, calls=%fused_computation.316 | loop fusion | bytes 9961472 | tf_op jit(solution)/shard_map/slice | solution.py:31
  219.9 6.8 %concatenate.93 = bf16[576,4,8,64]{0,3,2,1:T(8,128)(2,1)} concatenate(bf16[64,4,8,64]{0,3,2,1:T(8,128)(2,1)} %get-tuple-element.79, bf16[64,4,8,64]{0,3,2,1:T(8,128)(2,1)} %get-tuple-element.78, bf16[64,4,8,64]{0,3,2,1:T(8,128)(2,1)} %get-tuple-element.77, bf16[64,4,8,64]{0,3,2,1:T(8,128)(2,1)} %get-tuple-element.76, bf16[64,4,8,64]{0,3,2,1:T(8,128)(2,1)} %get-tuple-element.130, ...), dimensions={0} | concatenate | bytes 4718592 | tf_op jit(solution)/shard_map/concatenate | solution.py:30
  226.7 4.1 %fusion.118 = f32[4,8,64,32]{2,3,1,0:T(8,128)} fusion(bf16[576,4,8,64]{0,3,2,1:T(8,128)(2,1)} %concatenate.93, bf16[32,576,1,1]{1,0,2,3:T(8,128)(2,1)S(1)} %copy-done.29), kind=kOutput, calls=%fused_computation.276 | convolution fusion | flops 75497472 | bytes 2658304 | tf_op jit(solution)/shard_map/oc,cxzy->oxzy/dot_general | solution.py:35
  230.8 6.7 %concatenate.91 = bf16[576,4,8,64]{0,3,2,1:T(8,128)(2,1)} concatenate(bf16[64,4,8,64]{0,3,2,1:T(8,128)(2,1)} %get-tuple-element.87, bf16[64,4,8,64]{0,3,2,1:T(8,128)(2,1)} %get-tuple-element.86, bf16[64,4,8,64]{0,3,2,1:T(8,128)(2,1)} %get-tuple-element.85, bf16[64,4,8,64]{0,3,2,1:T(8,128)(2,1)} %get-tuple-element.84, bf16[64,4,8,64]{0,3,2,1:T(8,128)(2,1)S(1)} %fusion.24, ...), dimensions={0} | concatenate | bytes 4718592 | tf_op jit(solution)/shard_map/concatenate | solution.py:30
  237.4 4.1 %fusion.120 = f32[4,8,64,32]{2,3,1,0:T(8,128)} fusion(bf16[576,4,8,64]{0,3,2,1:T(8,128)(2,1)} %concatenate.91, bf16[32,576,1,1]{1,0,2,3:T(8,128)(2,1)S(1)} %copy-done.28), kind=kOutput, calls=%fused_computation.278 | convolution fusion | flops 75497472 | bytes 2658304 | tf_op jit(solution)/shard_map/oc,cxzy->oxzy/dot_general | solution.py:35
  241.6 6.4 %concatenate.90 = bf16[576,4,8,64]{0,3,2,1:T(8,128)(2,1)} concatenate(bf16[64,4,8,64]{0,3,2,1:T(8,128)(2,1)S(1)} %copy-done.13, bf16[64,4,8,64]{0,3,2,1:T(8,128)(2,1)S(1)} %get-tuple-element.93, bf16[64,4,8,64]{0,3,2,1:T(8,128)(2,1)S(1)} %get-tuple-element.92, bf16[64,4,8,64]{0,3,2,1:T(8,128)(2,1)S(1)} %get-tuple-element.91, bf16[64,4,8,64]{0,3,2,1:T(8,128)(2,1)} %get-tuple-element.129, ...), dimensions={0} | concatenate | bytes 4718592 | tf_op jit(solution)/shard_map/concatenate | solution.py:30
  248.0 3.5 fusion.27
  251.9 7.5 %broadcast_in_dim.36 = f32[32,4,2,8,2,64,2]{0,6,5,4,3,2,1:T(2,128)} broadcast(f32[32,4,8,64]{0,3,2,1:T(8,128)S(1)} %copy.195), dimensions={0,1,3,5} | broadcast | bytes 2359296 | tf_op jit(solution)/shard_map/broadcast_in_dim | solution.py:80
  259.4 6.3 %copy.196 = f32[32,8,16,128]{3,0,2,1:T(8,128)} copy(f32[32,8,16,128]{0,3,2,1:T(8,128)} %bitcast.671) | data formatting | bytes 4194304 | tf_op jit(solution)/shard_map/mul | solution.py:123
  265.8 4.6 %fusion.12 = (bf16[32,8,16,128]{3,0,2,1:T(8,128)(2,1)S(1)}, bf16[32,8,16,128]{3,0,2,1:T(8,128)(2,1)S(1)}) fusion(f32[32,8,16,128]{3,0,2,1:T(8,128)} %copy.196, f32[8,16,128,32]{2,3,1,0:T(8,128)} %get-tuple-element.151, f32[16,128]{1,0:T(8,128)S(1)} %broadcast_in_dim.32, bf16[32,8,16,128]{3,2,1,0:T(8,128)(2,1)S(1)} %copy-done.12, f32[32,8,16,128]{3,0,2,1:T(8,128)} %copy.188), kind=kLoop, calls=%fused_computation.30 | loop fusion | flops 9961472 | bytes 9445376 | tf_op jit(solution)/shard_map/convert_element_type | solution.py:124
  311.8 69.7 %all-reduce.7.cloned.1.call-done = (f32[32,32,3,3,3]{1,0,4,3,2:T(8,128)}, f32[64,32,3,3,3]{0,1,4,3,2:T(8,128)}) async-done(((f32[32,32,3,3,3]{1,0,4,3,2:T(8,128)}, f32[64,32,3,3,3]{0,1,4,3,2:T(8,128)}), (f32[32,32,3,3,3]{1,0,4,3,2:T(8,128)}, f32[64,32,3,3,3]{0,1,4,3,2:T(8,128)})) %all-reduce.7.cloned.1.call-update) | async-done | bytes 331792 | tf_op jit(solution)/shard_map/psum | solution.py:128
  (211 shorter events, 110.7 us)
Async XLA Ops:
  7.2 111.8 %copy-start = (bf16[32,64]{1,0:T(8,128)(2,1)S(1)}, bf16[32,64]{1,0:T(8,128)(2,1)}, u32[]{:S(2)}) copy-start(bf16[32,64]{1,0:T(8,128)(2,1)} %param.10) | copy-start | bytes 12292
  7.2 6.8 %copy-start.15 = (bf16[32,32,3,3,3]{1,0,4,3,2:T(8,128)(2,1)S(1)}, bf16[32,32,3,3,3]{1,0,4,3,2:T(8,128)(2,1)}, u32[]{:S(2)}) copy-start(bf16[32,32,3,3,3]{1,0,4,3,2:T(8,128)(2,1)} %param.8) | copy-start | bytes 165892
  7.2 7.4 %copy-start.16 = (bf16[64,32,3,3,3]{0,1,4,3,2:T(8,128)(2,1)S(1)}, bf16[64,32,3,3,3]{0,1,4,3,2:T(8,128)(2,1)}, u32[]{:S(2)}) copy-start(bf16[64,32,3,3,3]{0,1,4,3,2:T(8,128)(2,1)} %param.9) | copy-start | bytes 331780
  7.2 8.1 %copy-start.32 = (s32[1,2,16]{2,1,0:T(2,128)S(1)}, s32[1,2,16]{2,1,0:T(2,128)}, u32[]{:S(2)}) copy-start(s32[1,2,16]{2,1,0:T(2,128)} %param.7) | copy-start | bytes 388
  7.2 374.3 %all-reduce.7.cloned.1.call-start = ((), (), s32[]{:S(2)}) async-start(), calls=%async_computation | async-start | bytes 1769472 | tf_op jit(solution)/shard_map/psum | solution.py:128
  9.3 6.8 %collective-permute-start = (bf16[32,1,16,128]{3,0,2,1:T(8,128)(2,1)S(1)}, bf16[32,1,16,128]{3,0,2,1:T(8,128)(2,1)S(1)}, u32[]{:S(2)}, u32[]{:S(2)}) collective-permute-start(bf16[32,1,16,128]{3,0,2,1:T(8,128)(2,1)S(1)} %get-tuple-element.127), channel_id=1, source_target_pairs={{0,1},{1,2},{2,3},{3,4},{4,5},{5,6},{6,7},{7,8},{8,9},{9,10},{10,1... | collective-permute-start | bytes 393224 | tf_op jit(solution)/shard_map/ppermute | solution.py:14
  11.7 5.4 %collective-permute-start.1 = (bf16[32,1,16,128]{3,0,2,1:T(8,128)(2,1)S(1)}, bf16[32,1,16,128]{3,0,2,1:T(8,128)(2,1)S(1)}, u32[]{:S(2)}, u32[]{:S(2)}) collective-permute-start(bf16[32,1,16,128]{3,0,2,1:T(8,128)(2,1)S(1)} %get-tuple-element.128), channel_id=1, source_target_pairs={{1,0},{2,1},{3,2},{4,3},{5,4},{6,5},{7,6},{8,7},{9,8},{10,9},{11,1... | collective-permute-start | bytes 393224 | tf_op jit(solution)/shard_map/ppermute | solution.py:17
  16.1 7.7 %copy-start.19 = (bf16[32,1,16,128]{3,0,2,1:T(8,128)(2,1)}, bf16[32,1,16,128]{3,0,2,1:T(8,128)(2,1)S(1)}, u32[]{:S(2)}) copy-start(bf16[32,1,16,128]{3,0,2,1:T(8,128)(2,1)S(1)} %collective-permute-done) | copy-start | bytes 393220
  17.0 6.7 %copy-start.17 = (bf16[32,1,16,128]{3,0,2,1:T(8,128)(2,1)}, bf16[32,1,16,128]{3,0,2,1:T(8,128)(2,1)S(1)}, u32[]{:S(2)}) copy-start(bf16[32,1,16,128]{3,0,2,1:T(8,128)(2,1)S(1)} %collective-permute-done.1) | copy-start | bytes 393220
  19.0 10.4 %copy-start.2 = (bf16[32,10,18,130]{3,0,2,1:T(8,128)(2,1)}, bf16[32,10,18,130]{3,0,2,1:T(8,128)(2,1)S(1)}, u32[]{:S(2)}) copy-start(bf16[32,10,18,130]{3,0,2,1:T(8,128)(2,1)S(1)} %select_maximum_fusion.2) | copy-start | bytes 4492804
  54.9 25.7 %collective-permute-start.2 = (bf16[32,1,8,64]{0,3,2,1:T(8,128)(2,1)S(1)}, bf16[32,1,8,64]{0,3,2,1:T(8,128)(2,1)S(1)}, u32[]{:S(2)}, u32[]{:S(2)}) collective-permute-start(bf16[32,1,8,64]{0,3,2,1:T(8,128)(2,1)S(1)} %get-tuple-element.135), channel_id=1, source_target_pairs={{0,1},{1,2},{2,3},{3,4},{4,5},{5,6},{6,7},{7,8},{8,9},{9,10},{10,1... | collective-permute-start | bytes 98312 | tf_op jit(solution)/shard_map/ppermute | solution.py:14
  60.3 20.2 %collective-permute-start.3 = (bf16[32,1,8,64]{0,3,2,1:T(8,128)(2,1)S(1)}, bf16[32,1,8,64]{0,3,2,1:T(8,128)(2,1)S(1)}, u32[]{:S(2)}, u32[]{:S(2)}) collective-permute-start(bf16[32,1,8,64]{0,3,2,1:T(8,128)(2,1)S(1)} %get-tuple-element.136), channel_id=1, source_target_pairs={{1,0},{2,1},{3,2},{4,3},{5,4},{6,5},{7,6},{8,7},{9,8},{10,9},{11,1... | collective-permute-start | bytes 98312 | tf_op jit(solution)/shard_map/ppermute | solution.py:17
  88.8 6.6 %copy-start.4 = (bf16[32,4,8,64]{0,3,2,1:T(8,128)(2,1)}, bf16[32,4,8,64]{0,3,2,1:T(8,128)(2,1)S(1)}, u32[]{:S(2)}) copy-start(bf16[32,4,8,64]{0,3,2,1:T(8,128)(2,1)S(1)} %get-tuple-element.134) | copy-start | bytes 393220
  88.8 6.6 %copy-start.26 = (bf16[64,32,1,3,3]{0,1,4,3,2:T(8,128)(2,1)S(1)}, bf16[64,32,1,3,3]{0,1,4,3,2:T(8,128)(2,1)}, u32[]{:S(2)}) copy-start(bf16[64,32,1,3,3]{0,1,4,3,2:T(8,128)(2,1)} %get-tuple-element.145) | copy-start | bytes 110596
  98.4 6.5 %copy-start.25 = (bf16[64,32,1,3,3]{0,1,4,3,2:T(8,128)(2,1)S(1)}, bf16[64,32,1,3,3]{0,1,4,3,2:T(8,128)(2,1)}, u32[]{:S(2)}) copy-start(bf16[64,32,1,3,3]{0,1,4,3,2:T(8,128)(2,1)} %get-tuple-element.144) | copy-start | bytes 110596
  98.4 9.5 %copy-start.6 = (bf16[32,4,8,64]{0,3,2,1:T(8,128)(2,1)S(1)}, bf16[32,4,8,64]{0,3,2,1:T(8,128)(2,1)}, u32[]{:S(2)}) copy-start(bf16[32,4,8,64]{0,3,2,1:T(8,128)(2,1)} %get-tuple-element.133) | copy-start | bytes 393220
  107.9 6.6 %copy-start.30 = (bf16[64,32,1,3,3]{0,1,4,3,2:T(8,128)(2,1)S(1)}, bf16[64,32,1,3,3]{0,1,4,3,2:T(8,128)(2,1)}, u32[]{:S(2)}) copy-start(bf16[64,32,1,3,3]{0,1,4,3,2:T(8,128)(2,1)} %get-tuple-element.143) | copy-start | bytes 110596
  122.2 90.6 %collective-permute-start.4 = (bf16[64,1,8,64]{0,3,2,1:T(8,128)(2,1)}, bf16[64,1,8,64]{0,3,2,1:T(8,128)(2,1)S(1)}, u32[]{:S(2)}, u32[]{:S(2)}) collective-permute-start(bf16[64,1,8,64]{0,3,2,1:T(8,128)(2,1)} %get-tuple-element.131), channel_id=1, source_target_pairs={{0,1},{1,2},{2,3},{3,4},{4,5},{5,6},{6,7},{7,8},{8,9},{9,10},{10,1... | collective-permute-start | bytes 196616 | tf_op jit(solution)/shard_map/ppermute | solution.py:14
  125.3 87.5 %collective-permute-start.5 = (bf16[64,1,8,64]{0,3,2,1:T(8,128)(2,1)}, bf16[64,1,8,64]{0,3,2,1:T(8,128)(2,1)S(1)}, u32[]{:S(2)}, u32[]{:S(2)}) collective-permute-start(bf16[64,1,8,64]{0,3,2,1:T(8,128)(2,1)} %get-tuple-element.132), channel_id=1, source_target_pairs={{1,0},{2,1},{3,2},{4,3},{5,4},{6,5},{7,6},{8,7},{9,8},{10,9},{11,1... | collective-permute-start | bytes 196616 | tf_op jit(solution)/shard_map/ppermute | solution.py:17
  219.9 6.8 %copy-start.29 = (bf16[32,576,1,1]{1,0,2,3:T(8,128)(2,1)S(1)}, bf16[32,576,1,1]{1,0,2,3:T(8,128)(2,1)}, u32[]{:S(2)}) copy-start(bf16[32,576,1,1]{1,0,2,3:T(8,128)(2,1)} %reshape.96) | copy-start | bytes 110596
  230.7 6.7 %copy-start.28 = (bf16[32,576,1,1]{1,0,2,3:T(8,128)(2,1)S(1)}, bf16[32,576,1,1]{1,0,2,3:T(8,128)(2,1)}, u32[]{:S(2)}) copy-start(bf16[32,576,1,1]{1,0,2,3:T(8,128)(2,1)} %reshape.95) | copy-start | bytes 110596
  272.9 17.5 %collective-permute-start.6 = (bf16[32,1,16,128]{3,0,2,1:T(8,128)(2,1)}, bf16[32,1,16,128]{3,0,2,1:T(8,128)(2,1)S(1)}, u32[]{:S(2)}, u32[]{:S(2)}) collective-permute-start(bf16[32,1,16,128]{3,0,2,1:T(8,128)(2,1)} %get-tuple-element.123), channel_id=1, source_target_pairs={{0,1},{1,2},{2,3},{3,4},{4,5},{5,6},{6,7},{7,8},{8,9},{9,10},{10,1... | collective-permute-start | bytes 393224 | tf_op jit(solution)/shard_map/ppermute | solution.py:14
  274.2 16.2 %collective-permute-start.7 = (bf16[32,1,16,128]{3,0,2,1:T(8,128)(2,1)}, bf16[32,1,16,128]{3,0,2,1:T(8,128)(2,1)S(1)}, u32[]{:S(2)}, u32[]{:S(2)}) collective-permute-start(bf16[32,1,16,128]{3,0,2,1:T(8,128)(2,1)} %get-tuple-element.124), channel_id=1, source_target_pairs={{1,0},{2,1},{3,2},{4,3},{5,4},{6,5},{7,6},{8,7},{9,8},{10,9},{11,1... | collective-permute-start | bytes 393224 | tf_op jit(solution)/shard_map/ppermute | solution.py:17
  307.4 77.7 %copy-start.1 = (bf16[32,64]{1,0:T(8,128)(2,1)S(1)}, bf16[32,64]{1,0:T(8,128)(2,1)}, u32[]{:S(2)}) copy-start(bf16[32,64]{1,0:T(8,128)(2,1)} %param.10) | copy-start | bytes 12292
  (18 other events, 58.5 us)
Sparse Core Ops, SparseCore 0:
  290.5 90.9 all-reduce.6
where the time goes:
time: 398 us; the launch traced here: 392 us
  local copies, waits for them, and re-layouts  130 us (33%)
  waiting for transfers between devices  70.7 us (18%)
  blocking collectives  63.2 us (16%)
  matrix products  60.6 us (15%)
  other arithmetic  34.8 us (9%)
  starting transfers between devices  17.9 us (4%)
  between operations  15.1 us (4%)
    psum x1, waiting for transfers between devices, per_device(): lax.psum((grad_fine, grad_coarse, grad_up), 'gx')  69.7 us
    psum x1, blocking collectives, per_device(): lax.psum((grad_fine, grad_coarse, grad_up), 'gx')  63.2 us
    concatenate x8, local copies, waits for them, and re-layouts, conv_rows(): jnp.concatenate([slab[:, :, j:j + extent_z, k:k + extent_y] for j in rang...  42.7 us
    dot_general x12, matrix products, conv_rows(): jnp.einsum('oc,cxzy->oxzy', taps, stacked, preferred_element_type=jnp.flo...  34.7 us
    unnamed x85, local copies, waits for them, and re-layouts  27.5 us
    dot_general x54, matrix products, weight_grad(): jnp.einsum('oxzy,cxzy->oc', grad, window, preferred_element_type=jnp.floa...  22 us
    reduce_sum x2, other arithmetic, pool_sum(): values.reshape(chans, size_x // 2, 2, size_z // 2, 2, size_y // 2, 2)  18.4 us
    broadcast_in_dim x2, local copies, waits for them, and re-layouts, spread(): jnp.broadcast_to(values[:, :, None, :, None, :, None], (chans, size_x, 2,...  15 us
  transfers between devices with their start and end apart: 9, of which 2 were waited for; matrix products, arithmetic and copies ran while one was open for 20% of the time, Pallas kernels for 0%

commit v1 on v0

v1 whole, which is shorter than its diff:
```python
import functools
import math

import jax
import jax.numpy as jnp
import numpy as np
from jax import lax
from jax.experimental import pallas as pl
from jax.experimental.pallas import tpu as pltpu
from jax.sharding import PartitionSpec as P

F32 = jnp.float32
BF16 = jnp.bfloat16
VMEM_LIMIT = 48 * 1024 * 1024
MESH = pl.DeviceIdType.MESH
ALONG = 4


def dot(a, b):
    return jnp.dot(a, b, preferred_element_type=F32)


def dot_nt(a, b):
    return lax.dot_general(a, b, (((1,), (1,)), ((), ())), preferred_element_type=F32)


def halves(value):
    high = value.astype(BF16)
    return high, (value - high.astype(F32)).astype(BF16)


def pool_matrix(size_y):
    cell = np.arange(4 * size_y)
    coarse = np.arange(size_y)
    same_z = (cell // size_y // 2)[:, None] == (coarse // (size_y // 2))[None]
    same_y = (cell % size_y // 2)[:, None] == (coarse % (size_y // 2))[None]
    return (same_z & same_y).astype(np.float32)


def gather_fine(value, size_y, cols_ref, row):
    chans, length = value.shape
    wide = value.astype(F32)
    spot = lax.broadcasted_iota(jnp.int32, (chans, length), 1) % size_y
    before = jnp.where(spot == 0, 0.0, pltpu.roll(wide, 1, 1)).astype(BF16)
    after = jnp.where(spot == size_y - 1, 0.0, pltpu.roll(wide, length - 1, 1)).astype(BF16)
    edge = jnp.zeros((chans, size_y), BF16)
    for k, shifted in enumerate((before, value, after)):
        low = pl.ds(row + k * chans, chans)
        mid = pl.ds(row + (3 + k) * chans, chans)
        high = pl.ds(row + (6 + k) * chans, chans)
        cols_ref[low, :size_y] = edge
        cols_ref[low, size_y:] = shifted[:, :-size_y]
        cols_ref[mid, :] = shifted
        cols_ref[high, : length - size_y] = shifted[:, size_y:]
        cols_ref[high, length - size_y :] = edge


def gather_coarse(value, size_y, cols_ref, row):
    chans, length = value.shape
    wide = value.astype(F32)
    cell = lax.broadcasted_iota(jnp.int32, (chans, length), 1)
    spot = cell % size_y
    for j in range(3):
        for k in range(3):
            shift = (j - 1) * size_y + (k - 1)
            rolled = pltpu.roll(wide, (-shift) % length, 1) if shift else wide
            if k == 0:
                rolled = jnp.where(spot == 0, 0.0, rolled)
            if k == 2:
                rolled = jnp.where(spot == size_y - 1, 0.0, rolled)
            if j == 0:
                rolled = jnp.where(cell < size_y, 0.0, rolled)
            if j == 2:
                rolled = jnp.where(cell >= length - size_y, 0.0, rolled)
            cols_ref[pl.ds(row + (3 * j + k) * chans, chans), :] = rolled.astype(BF16)


def gather_planes(gather, low_ref, mid_ref, high_ref, chans, size_y, cols_ref):
    planes = mid_ref.shape[0] // chans
    depth = 9 * chans
    gather(low_ref[...], size_y, cols_ref, 0)
    gather(high_ref[...], size_y, cols_ref, (planes + 1) * depth)

    def body(plane, carry):
        start = pl.multiple_of(plane * chans, chans)
        row = pl.multiple_of((plane + 1) * depth, depth)
        gather(mid_ref[pl.ds(start, chans), :], size_y, cols_ref, row)
        return carry

    lax.fori_loop(0, planes, body, 0)


def sum_pairs(value, chans):
    count = value.shape[0] // chans
    return jnp.concatenate(
        [
            value[(2 * i) * chans : (2 * i + 1) * chans]
            + value[(2 * i + 1) * chans : (2 * i + 2) * chans]
            for i in range(count // 2)
        ],
        axis=0,
    )


def repeat_pairs(value, chans):
    count = value.shape[0] // chans
    parts = [value[i // 2 * chans : (i // 2 + 1) * chans] for i in range(2 * count)]
    return jnp.concatenate(parts, axis=0)


def sigmoid(value):
    return 1.0 / (1.0 + jnp.exp(-value))


def fine_forward(
    size_y, low_ref, mid_ref, high_ref, taps_ref, mask_ref, pool_ref,
    hidden_ref, slope_ref, pooled_ref, cols_ref,
):
    chans = low_ref.shape[0]
    length = mid_ref.shape[1]
    gather_planes(gather_fine, low_ref, mid_ref, high_ref, chans, size_y, cols_ref)
    depth = 9 * chans
    wide = 4 * size_y
    for group in range(mid_ref.shape[0] // chans // ALONG):
        rows = slice(group * ALONG * depth, (group * ALONG + ALONG + 2) * depth)
        held = slice(group * ALONG * chans, (group + 1) * ALONG * chans)
        out = slice(group * ALONG // 2 * chans, (group + 1) * ALONG // 2 * chans)
        for step in range(length // wide):
            lanes = slice(step * wide, (step + 1) * wide)
            pre = dot(taps_ref[...], cols_ref[rows, lanes])
            mask = mask_ref[:, lanes]
            sigma = sigmoid(pre)
            hidden = (pre * sigma * mask).astype(BF16)
            hidden_ref[held, lanes] = hidden
            slope_ref[held, lanes] = sigma * (1.0 + pre * (1.0 - sigma)) * mask
            pooled = sum_pairs(dot(hidden, pool_ref[...]), chans) * 0.125
            pooled_ref[out, step * size_y : (step + 1) * size_y] = pooled.astype(BF16)


def lift_pool(size_y, chans, cotangent_ref, mask_ref, pool_ref, lift_ref):
    wide = 4 * size_y
    for step in range(cotangent_ref.shape[1] // wide):
        lanes = slice(step * wide, (step + 1) * wide)
        value = (cotangent_ref[:, lanes].astype(F32) * mask_ref[:, lanes]).astype(BF16)
        lift_ref[:, step * size_y : (step + 1) * size_y] = sum_pairs(
            dot(value, pool_ref[...]), chans
        )


def coarse_forward(
    size_y, low_ref, mid_ref, high_ref, taps_ref, mask_ref, lift_ref, back_ref,
    hidden_ref, grad_ref, cols_ref,
):
    chans = low_ref.shape[0]
    gather_planes(gather_coarse, low_ref, mid_ref, high_ref, chans, size_y, cols_ref)
    pre = dot(taps_ref[...], cols_ref[...])
    mask = mask_ref[...]
    sigma = sigmoid(pre)
    hidden_ref[...] = (pre * sigma * mask).astype(BF16)
    high, low = halves(lift_ref[...])
    lifted = dot(back_ref[...], high) + dot(back_ref[...], low)
    slope = sigma * (1.0 + pre * (1.0 - sigma))
    grad_ref[...] = (lifted * mask * slope).astype(BF16)


def coarse_outputs(
    size_y, low_ref, mid_ref, high_ref, hidden_ref, grad_ref, lift_ref, up_ref, fine_ref,
    mask_ref, spread_ref, net_ref, grad_coarse_ref, grad_up_ref, cols_ref,
):
    chans = low_ref.shape[0]
    planes = mid_ref.shape[0] // chans
    inner = hidden_ref.shape[0] // planes
    depth = 9 * chans
    gather_planes(gather_coarse, low_ref, mid_ref, high_ref, chans, size_y // 2, cols_ref)
    lifted = dot(up_ref[...], hidden_ref[...])
    high, low = halves(lifted)
    wide = 4 * size_y
    for step in range(fine_ref.shape[1] // wide):
        lanes = slice(step * wide, (step + 1) * wide)
        coarse = slice(step * size_y, (step + 1) * size_y)
        spread = dot(high[:, coarse], spread_ref[...]) + dot(low[:, coarse], spread_ref[...])
        value = fine_ref[:, lanes].astype(F32) + mask_ref[:, lanes] * repeat_pairs(spread, chans)
        net_ref[:, lanes] = value.astype(BF16)
    lift_high, lift_low = halves(lift_ref[...])
    grad_coarse = 0.0
    grad_up = 0.0
    for x in range(planes):
        hidden = hidden_ref[x * inner : (x + 1) * inner, :]
        held = slice(x * chans, (x + 1) * chans)
        grad_up += dot_nt(lift_high[held], hidden) + dot_nt(lift_low[held], hidden)
        grad_coarse += dot_nt(
            cols_ref[x * depth : (x + 3) * depth, :], grad_ref[x * inner : (x + 1) * inner, :]
        )
    grad_coarse_ref[...] = grad_coarse
    grad_up_ref[...] = grad_up


def coarse_backward(
    size_y, low_ref, mid_ref, high_ref, taps_ref, cotangent_ref, slope_ref, spread_ref,
    grad_ref, cols_ref,
):
    inner = low_ref.shape[0]
    planes = mid_ref.shape[0] // inner
    chans = cotangent_ref.shape[0] // (2 * planes)
    gather_planes(gather_coarse, low_ref, mid_ref, high_ref, inner, size_y // 2, cols_ref)
    high, low = halves(dot(taps_ref[...], cols_ref[...]) * 0.125)
    wide = 4 * size_y
    for step in range(cotangent_ref.shape[1] // wide):
        lanes = slice(step * wide, (step + 1) * wide)
        coarse = slice(step * size_y, (step + 1) * size_y)
        spread = dot(high[:, coarse], spread_ref[...]) + dot(low[:, coarse], spread_ref[...])
        value = cotangent_ref[:, lanes].astype(F32) + repeat_pairs(spread, chans)
        grad_ref[:, lanes] = (value * slope_ref[:, lanes]).astype(BF16)


def fine_backward(
    size_y, low_ref, mid_ref, high_ref, taps_ref, features_ref,
    grad_features_ref, grad_fine_ref, cols_ref, framed_ref,
):
    chans = low_ref.shape[0]
    planes = mid_ref.shape[0] // chans
    length = mid_ref.shape[1]
    depth = 9 * chans
    gather_planes(gather_fine, low_ref, mid_ref, high_ref, chans, size_y, cols_ref)
    empty = jnp.zeros((2 * chans, length), BF16)
    framed_ref[: 2 * chans, :] = empty
    framed_ref[2 * chans : (planes + 2) * chans, :] = features_ref[...]
    framed_ref[(planes + 2) * chans :, :] = empty
    wide = 4 * size_y
    for group in range(planes // ALONG):
        rows = slice(group * ALONG * depth, (group * ALONG + ALONG + 2) * depth)
        held = slice(group * ALONG * chans, (group + 1) * ALONG * chans)
        for step in range(length // wide):
            lanes = slice(step * wide, (step + 1) * wide)
            grad_features_ref[held, lanes] = dot(taps_ref[...], cols_ref[rows, lanes])
    total = 0.0
    for plane in range(planes + 2):
        total += dot_nt(
            cols_ref[plane * depth : (plane + 1) * depth, :],
            framed_ref[plane * chans : (plane + 3) * chans, :],
        )
    grad_fine_ref[...] = total


def sum_over(
    count, chunk, factor, fine_ref, coarse_ref, up_ref, out_ref,
    packed, slots, part, whole, send_a, recv_a, send_b, recv_b,
):
    me = lax.axis_index("gx")
    barrier = pltpu.get_barrier_semaphore()

    def peer(d):
        return lax.rem(me + d, count)

    def greet(d, carry):
        pl.semaphore_signal(barrier, inc=1, device_id={"gx": peer(d)}, device_id_type=MESH)
        return carry

    lax.fori_loop(1, count, greet, 0)

    fine_rows, fine_cols = fine_ref.shape
    half = coarse_ref.shape[0] // 2
    coarse_cols = coarse_ref.shape[1]
    packed[...] = jnp.zeros(packed.shape, BF16)
    packed[:fine_rows, :fine_cols] = fine_ref[...].astype(BF16)
    packed[fine_rows : fine_rows + half, :coarse_cols] = coarse_ref[:half, :].astype(BF16)
    packed[fine_rows : fine_rows + half, coarse_cols : 2 * coarse_cols] = coarse_ref[
        half:, :
    ].astype(BF16)
    first = fine_rows + half
    packed[first : first + up_ref.shape[0], : up_ref.shape[1]] = up_ref[...].astype(BF16)
    pl.semaphore_wait(barrier, count - 1)

    def rows_of(index):
        return pl.ds(pl.multiple_of(index * chunk, chunk), chunk)

    def scatter(d):
        return pltpu.make_async_remote_copy(
            src_ref=packed.at[rows_of(peer(d))],
            dst_ref=slots.at[d],
            send_sem=send_a.at[d],
            recv_sem=recv_a.at[d],
            device_id={"gx": peer(d)},
            device_id_type=MESH,
        )

    def spread(d):
        return pltpu.make_async_remote_copy(
            src_ref=part,
            dst_ref=whole.at[rows_of(me)],
            send_sem=send_b.at[d],
            recv_sem=recv_b.at[d],
            device_id={"gx": peer(d)},
            device_id_type=MESH,
        )

    def start(copy):
        def body(d, carry):
            copy(d).start()
            return carry

        lax.fori_loop(1, count, body, 0)

    start(scatter)

    def add(d, total):
        scatter(d).wait_recv()
        return total + slots[d].astype(F32)

    total = lax.fori_loop(1, count, add, packed[rows_of(me), :].astype(F32))
    part[...] = (total * factor).astype(BF16)
    start(spread)
    whole[rows_of(me), :] = part[...]

    def finish(d, carry):
        scatter(d).wait_send()
        spread(d).wait_send()
        spread(d).wait_recv()
        return carry

    lax.fori_loop(1, count, finish, 0)
    out_ref[...] = whole[...].astype(F32)


def call(kernel, out_shape, scratch, *args, **params):
    flops = params.pop("flops", 0)
    size = sum(math.prod(a.shape) * a.dtype.itemsize for a in args)
    return pl.pallas_call(
        kernel,
        out_shape=out_shape,
        in_specs=[pl.BlockSpec(memory_space=pltpu.VMEM)] * len(args),
        out_specs=jax.tree.map(lambda _: pl.BlockSpec(memory_space=pltpu.VMEM), out_shape),
        scratch_shapes=scratch,
        compiler_params=pltpu.CompilerParams(vmem_limit_bytes=VMEM_LIMIT, **params),
        cost_estimate=pl.CostEstimate(flops=flops, bytes_accessed=2 * size, transcendentals=0),
    )(*args)


def banded(weight):
    outs, ins = weight.shape[:2]
    depth = 9 * ins
    taps = weight.transpose(0, 2, 3, 4, 1).reshape(outs, 3 * depth)
    return jnp.concatenate(
        [jnp.pad(taps, ((0, 0), (x * depth, (ALONG - 1 - x) * depth))) for x in range(ALONG)],
        axis=0,
    )


def flip_weight(weight):
    return jnp.flip(weight, (2, 3, 4)).transpose(1, 0, 2, 3, 4)


def planes_first(values):
    chans, size_x, size_z, size_y = values.shape
    return values.transpose(1, 0, 2, 3).reshape(size_x * chans, size_z * size_y)


def channels_first(values, chans, size_z, size_y):
    return values.reshape(-1, chans, size_z, size_y).transpose(1, 0, 2, 3)


def faces(values, chans):
    count = lax.axis_size("gx")
    forward = [(i, i + 1) for i in range(count - 1)]
    backward = [(target, source) for source, target in forward]
    low = lax.ppermute(values[-chans:], "gx", forward)
    high = lax.ppermute(values[:chans], "gx", backward)
    return low, values, high


def expand_row(blocks, times):
    values = blocks.astype(F32)[0]
    size_z, size_y = values.shape
    values = jnp.broadcast_to(values[:, None, :, None], (size_z, times, size_y, times))
    return values.reshape(1, size_z * times * size_y * times)


def per_device(features, active_blocks, weight_fine, weight_coarse, weight_up, cotangent):
    chans, size_x, size_z, size_y = features.shape
    inner = weight_coarse.shape[0]
    count = lax.axis_size("gx")
    factor = 1.0 / math.sqrt(size_x * count * size_z * size_y)
    length = size_z * size_y
    half_x, coarse_length = size_x // 2, length // 4
    shape = jax.ShapeDtypeStruct

    fine_mask = expand_row(active_blocks, 8)
    coarse_mask = expand_row(active_blocks, 4)
    pool = jnp.asarray(pool_matrix(size_y), BF16)
    spread = jnp.asarray(pool_matrix(size_y).T, BF16)
    diagonal = jnp.eye(half_x, dtype=BF16)
    up_blocks = jnp.kron(diagonal, weight_up)
    back_blocks = jnp.kron(diagonal, weight_up.T)

    rows = planes_first(features)
    fine_faces = faces(rows, chans)
    cotangent_rows = planes_first(cotangent)

    fine_cols = pltpu.VMEM(((size_x + 2) * 9 * chans, length), BF16)
    hidden_fine, slope_fine, pooled = call(
        functools.partial(fine_forward, size_y),
        (
            shape((size_x * chans, length), BF16),
            shape((size_x * chans, length), F32),
            shape((half_x * chans, coarse_length), BF16),
        ),
        [fine_cols],
        *fine_faces, banded(weight_fine), fine_mask, pool,
    )
    pooled_faces = faces(pooled, chans)
    grad_lift = call(
        functools.partial(lift_pool, size_y, chans),
        shape((half_x * chans, coarse_length), F32),
        [],
        cotangent_rows, fine_mask, pool,
    )
    coarse_cols = pltpu.VMEM(((half_x + 2) * 9 * chans, coarse_length), BF16)
    hidden_coarse, grad_pre_coarse = call(
        functools.partial(coarse_forward, size_y // 2),
        (
            shape((half_x * inner, coarse_length), BF16),
            shape((half_x * inner, coarse_length), BF16),
        ),
        [coarse_cols],
        *pooled_faces, banded(weight_coarse), coarse_mask, grad_lift, back_blocks,
    )
    grad_faces = faces(grad_pre_coarse, inner)
    net_rows, grad_coarse, grad_up = call(
        functools.partial(coarse_outputs, size_y),
        (
            shape((size_x * chans, length), BF16),
            shape((27 * chans, inner), F32),
            shape((chans, inner), F32),
        ),
        [coarse_cols],
        *pooled_faces, hidden_coarse, grad_pre_coarse, grad_lift, up_blocks, hidden_fine,
        fine_mask, spread,
    )
    grad_pre_fine = call(
        functools.partial(coarse_backward, size_y),
        shape((size_x * chans, length), BF16),
        [pltpu.VMEM(((half_x + 2) * 9 * inner, coarse_length), BF16)],
        *grad_faces, banded(flip_weight(weight_coarse)), cotangent_rows, slope_fine, spread,
    )
    grad_fine_faces = faces(grad_pre_fine, chans)
    net_output = channels_first(net_rows, chans, size_z, size_y)
    grad_rows, grad_fine = call(
        functools.partial(fine_backward, size_y),
        (shape((size_x * chans, length), F32), shape((9 * chans, 3 * chans), F32)),
        [fine_cols, pltpu.VMEM(((size_x + 4) * chans, length), BF16)],
        *grad_fine_faces, banded(flip_weight(weight_fine)), rows,
    )
    used = 9 * chans + (27 * chans + 1) // 2 + chans
    chunk = -(-used // (16 * count)) * 16
    lanes = max(2 * inner, 3 * chans)
    sums = call(
        functools.partial(sum_over, count, chunk, factor),
        shape((count * chunk, lanes), F32),
        [
            pltpu.VMEM((count * chunk, lanes), BF16),
            pltpu.VMEM((count, chunk, lanes), BF16),
            pltpu.VMEM((chunk, lanes), BF16),
            pltpu.VMEM((count * chunk, lanes), BF16),
            pltpu.SemaphoreType.DMA((count,)),
            pltpu.SemaphoreType.DMA((count,)),
            pltpu.SemaphoreType.DMA((count,)),
            pltpu.SemaphoreType.DMA((count,)),
        ],
        grad_fine, grad_coarse, grad_up,
        collective_id=0, has_side_effects=True,
    )
    grad_features = channels_first(grad_rows, chans, size_z, size_y)
    fine_rows, half = 9 * chans, 27 * chans // 2
    grad_fine = sums[:fine_rows, : 3 * chans].reshape(3, 3, chans, 3, chans)
    grad_fine = jnp.flip(grad_fine, (0, 1)).transpose(2, 4, 3, 0, 1)
    grad_coarse = sums[fine_rows : fine_rows + half, : 2 * inner]
    grad_coarse = jnp.concatenate([grad_coarse[:, :inner], grad_coarse[:, inner:]], axis=0)
    grad_coarse = grad_coarse.reshape(3, 3, 3, chans, inner).transpose(4, 3, 0, 1, 2)
    grad_up = sums[fine_rows + half : fine_rows + half + chans, :inner]
    return (net_output, grad_features, grad_fine, grad_coarse, grad_up)


def solution(mesh):
    return jax.shard_map(
        per_device,
        mesh=mesh,
        in_specs=(
            P(None, ("groups", "gx"), None, None),
            P(("groups", "gx"), None, None),
            P(),
            P(),
            P(),
            P(None, ("groups", "gx"), None, None),
        ),
        out_specs=(
            P(None, ("groups", "gx"), None, None),
            P(None, ("groups", "gx"), None, None),
            P("groups", None, None, None, None),
            P("groups", None, None, None, None),
            P("groups", None),
        ),
        check_vma=False,
    )
```

time: 398 us -> 103 us (0.26); the launches traced: 392 us -> 102 us
  local copies, waits for them, and re-layouts: 130 us -> 31.5 us
  waiting for transfers between devices: 70.7 us -> 1.75 us
  blocking collectives: 63.2 us -> 0 us
  matrix products: 60.6 us -> 0 us
  Pallas kernels: 0 us -> 41.3 us
  other arithmetic: 34.8 us -> 4.68 us
  between operations: 15.1 us -> 1.04 us
    psum x1 -> x0, waiting for transfers between devices: 69.7 us -> none  [per_device(): lax.psum((grad_fine, grad_coarse, grad_up), 'gx')]
    psum x1 -> x0, blocking collectives: 63.2 us -> none  [per_device(): lax.psum((grad_fine, grad_coarse, grad_up), 'gx')]
    dot_general x69 -> x0, matrix products: 60.6 us -> none  [the longest x12 34.7 us: conv_rows(): jnp.einsum('oc,cxzy->oxzy', taps, stacked, preferred_element_type=jnp.flo...]
    concatenate x8 -> x0, local copies, waits for them, and re-layouts: 42.7 us -> none  [conv_rows(): jnp.concatenate([slab[:, :, j:j + extent_z, k:k + extent_y] for j in rang...]
    pallas_call x0 -> x7, Pallas kernels: none -> 41.3 us  [call(): pl.pallas_call(kernel, out_shape=out_shape, in_specs=[pl.BlockSpec(memory...]
    reduce_sum x2 -> x0, other arithmetic: 18.4 us -> none  [pool_sum(): values.reshape(chans, size_x // 2, 2, size_z // 2, 2, size_y // 2, 2)]
    broadcast_in_dim x6 -> x2, local copies, waits for them, and re-layouts: 15.4 us -> 0.15 us  [expand_row(): jnp.broadcast_to(values[:, None, :, None], (size_z, times, size_y, times))]
    slice x10 -> x7, local copies, waits for them, and re-layouts: 14.2 us -> 2.44 us  [the longest x4 1.7 us: faces(): high = lax.ppermute(values[:chans], 'gx', backward)]
  transfers between devices with their start and end apart: 9 -> 8, of which waited for: 2 -> 1; matrix products, arithmetic and copies ran while one was open for 20% -> 15% of each run, Pallas kernels for 0% -> 3%
where the time goes in v1:
time: 103 us; the launch traced here: 102 us
  Pallas kernels  41.3 us (40%)
  local copies, waits for them, and re-layouts  31.5 us (31%)
  starting transfers between devices  21.5 us (21%)
  other arithmetic  4.68 us (5%)
  waiting for transfers between devices  1.75 us (2%)
  between operations  1.04 us (1%)
    pallas_call x7, Pallas kernels, call(): pl.pallas_call(kernel, out_shape=out_shape, in_specs=[pl.BlockSpec(memory...  41.3 us
    unnamed x55, local copies, waits for them, and re-layouts  17.2 us
    ppermute x4, starting transfers between devices, faces(): low = lax.ppermute(values[-chans:], 'gx', forward)  16.2 us
    ppermute x4, starting transfers between devices, faces(): high = lax.ppermute(values[:chans], 'gx', backward)  5.34 us
    transpose x2, local copies, waits for them, and re-layouts, channels_first(): return values.reshape(-1, chans, size_z, size_y).transpose(1, 0, 2, 3)  2.82 us
    concatenate x4, other arithmetic, banded(): jnp.concatenate([jnp.pad(taps, ((0, 0), (x * depth, (ALONG - 1 - x) * dep...  2.29 us
  transfers between devices with their start and end apart: 8, of which 1 were waited for; matrix products, arithmetic and copies ran while one was open for 15% of the time, Pallas kernels for 3%

profile of v1, /device:TPU:0, one launch (start us, length us, event | category | flops | bytes accessed | tf_op | source)
XLA Modules:
  0.0 101.8 jit_solution(14044176040088198501)
XLA Ops:
  2.4 2.4 %collective-permute-start = (bf16[32,2048]{1,0:T(8,128)(2,1)}, bf16[32,2048]{1,0:T(8,128)(2,1)S(1)}, u32[]{:S(2)}, u32[]{:S(2)}) collective-permute-start(bf16[32,2048]{1,0:T(8,128)(2,1)} %bitcast.60), channel_id=1, source_target_pairs={{0,1},{1,2},{2,3},{3,4},{4,5},{5,6},{6,7},{7,8},{8,9},{9,10},{10,1... | collective-permute-start | bytes 393224 | tf_op jit(solution)/shard_map/ppermute | solution.py:366
  5.4 1.3 %collective-permute-start.1 = (bf16[32,2048]{1,0:T(8,128)(2,1)}, bf16[32,2048]{1,0:T(8,128)(2,1)S(1)}, u32[]{:S(2)}, u32[]{:S(2)}) collective-permute-start(bf16[32,2048]{1,0:T(8,128)(2,1)} %bitcast.59), channel_id=1, source_target_pairs={{1,0},{2,1},{3,2},{4,3},{5,4},{6,5},{7,6},{8,7},{9,8},{10,9},{11,1... | collective-permute-start | bytes 393224 | tf_op jit(solution)/shard_map/ppermute | solution.py:367
  7.7 1.1 %copy.24 = bf16[32,3,3,3,32]{4,3,2,1,0:T(4,128)(2,1)S(1)} copy(bf16[32,3,3,3,32]{4,0,3,2,1:T(8,128)(2,1)} %bitcast.78) | data formatting | bytes 110592 | tf_op jit(solution)/shard_map/transpose | solution.py:342
  10.2 1.2 %copy.33 = bf16[32,3,3,3,64]{4,3,2,1,0:T(4,128)(2,1)S(1)} copy(bf16[32,3,3,3,64]{4,0,3,2,1:T(8,128)(2,1)} %reverse_bitcast_fusion.1) | data formatting | bytes 221184 | tf_op jit(solution)/shard_map/transpose;transpose | solution.py:342
  11.6 1.1 %fusion.22.taps_ref = bf16[128,3456]{1,0:T(8,128)(2,1)} fusion(bf16[32,1728]{1,0:T(8,128)(2,1)S(1)} %reshape.76), kind=kLoop, calls=%fused_computation.44 | loop fusion | flops 8847360 | bytes 995328 | tf_op jit(solution)/shard_map/concatenate | solution.py:343
  14.6 5.9 %shard_map.119 = (bf16[256,2048]{1,0:T(8,128)(2,1)S(1)}, f32[256,2048]{1,0:T(8,128)S(1)}, bf16[128,512]{1,0:T(8,128)(2,1)S(1)}) custom-call(bf16[32,2048]{1,0:T(8,128)(2,1)S(1)} %collective-permute-done.low_ref, bf16[256,2048]{1,0:T(8,128)(2,1)S(1)} %bitcast.65, bf16[32,2048]{1,0:T(8,128)(2,1)S(1)} %collective-permute-done.1.high_ref, ...), custom_call_target="tpu_custom_call" | custom-call | bytes 3784704 | tf_op jit(solution)/shard_map/pallas_call | solution.py:328
  20.5 1.3 %copy-done.1 = f32[256,2048]{1,0:T(8,128)} copy-done((f32[256,2048]{1,0:T(8,128)}, f32[256,2048]{1,0:T(8,128)S(1)}, u32[]{:S(2)}) %copy-start.1) | copy-done | bytes 2097176
  24.1 5.1 %collective-permute-start.2 = (bf16[32,512]{1,0:T(8,128)(2,1)}, bf16[32,512]{1,0:T(8,128)(2,1)S(1)}, u32[]{:S(2)}, u32[]{:S(2)}) collective-permute-start(bf16[32,512]{1,0:T(8,128)(2,1)} %get-tuple-element.39), channel_id=1, source_target_pairs={{0,1},{1,2},{2,3},{3,4},{4,5},{5,6},{6,7},{7,8},{8,9},{9,10},{10,1... | collective-permute-start | bytes 98312 | tf_op jit(solution)/shard_map/ppermute | solution.py:366
  29.3 1.3 %collective-permute-start.3 = (bf16[32,512]{1,0:T(8,128)(2,1)}, bf16[32,512]{1,0:T(8,128)(2,1)S(1)}, u32[]{:S(2)}, u32[]{:S(2)}) collective-permute-start(bf16[32,512]{1,0:T(8,128)(2,1)} %get-tuple-element.38), channel_id=1, source_target_pairs={{1,0},{2,1},{3,2},{4,3},{5,4},{6,5},{7,6},{8,7},{9,8},{10,9},{11,1... | collective-permute-start | bytes 98312 | tf_op jit(solution)/shard_map/ppermute | solution.py:367
  31.6 1.4 %copy.29 = bf16[8,32,16,128]{3,2,1,0:T(8,128)(2,1)S(1)} copy(bf16[8,32,16,128]{3,2,0,1:T(8,128)(2,1)} %bitcast.77) | data formatting | bytes 2097152 | tf_op jit(solution)/shard_map/transpose | solution.py:355
  33.8 1.1 %mul.51 = bf16[256,128]{0,1:T(8,128)(2,1)S(1)} reshape(bf16[4,64,4,32]{1,0,3,2:T(4,128)(2,1)} %broadcast_multiply_fusion.1) | data formatting | bytes 131072 | tf_op jit(solution)/shard_map/jit(kron)/mul | solution.py:393
  40.1 1.5 %shard_map.121 = (bf16[256,512]{1,0:T(8,128)(2,1)S(1)}, bf16[256,512]{1,0:T(8,128)(2,1)S(1)}) custom-call(bf16[32,512]{1,0:T(8,128)(2,1)S(1)} %copy-done.15, bf16[128,512]{1,0:T(8,128)(2,1)S(1)} %copy-done.7, bf16[32,512]{1,0:T(8,128)(2,1)S(1)} %copy-done.18, bf16[256,1728]{1,0:T(8,128)(2,1)S(1)} %fusion.13.taps_ref, f32[1,512]{1,0:T(1,128)S(1)} %reshape.73.mask_ref, ...), custom_call_target="tpu_custom_call" | custom-call | bytes 2822144 | tf_op jit(solution)/shard_map/pallas_call | solution.py:328
  42.3 4.3 %collective-permute-start.4 = (bf16[64,512]{1,0:T(8,128)(2,1)S(1)}, bf16[64,512]{1,0:T(8,128)(2,1)S(1)}, u32[]{:S(2)}, u32[]{:S(2)}) collective-permute-start(bf16[64,512]{1,0:T(8,128)(2,1)S(1)} %get-tuple-element.37), channel_id=1, source_target_pairs={{0,1},{1,2},{2,3},{3,4},{4,5},{5,6},{6,7},{7,8},{8,9},{9,10},{10,1... | collective-permute-start | bytes 196616 | tf_op jit(solution)/shard_map/ppermute | solution.py:366
  46.6 1.3 %collective-permute-start.5 = (bf16[64,512]{1,0:T(8,128)(2,1)S(1)}, bf16[64,512]{1,0:T(8,128)(2,1)S(1)}, u32[]{:S(2)}, u32[]{:S(2)}) collective-permute-start(bf16[64,512]{1,0:T(8,128)(2,1)S(1)} %get-tuple-element.36), channel_id=1, source_target_pairs={{1,0},{2,1},{3,2},{4,3},{5,4},{6,5},{7,6},{8,7},{9,8},{10,9},{11,1... | collective-permute-start | bytes 196616 | tf_op jit(solution)/shard_map/ppermute | solution.py:367
  48.9 1.2 %copy-done.5 = bf16[256,2048]{1,0:T(8,128)(2,1)S(1)} copy-done((bf16[256,2048]{1,0:T(8,128)(2,1)S(1)}, bf16[256,2048]{1,0:T(8,128)(2,1)}, u32[]{:S(2)}) %copy-start.5) | copy-done | bytes 1048600
  54.4 2.3 %shard_map.122 = (bf16[256,2048]{1,0:T(8,128)(2,1)S(1)}, f32[864,64]{1,0:T(8,128)S(1)}, f32[32,64]{1,0:T(8,128)S(1)}) custom-call(bf16[32,512]{1,0:T(8,128)(2,1)S(1)} %copy-done.16, bf16[128,512]{1,0:T(8,128)(2,1)S(1)} %copy-done.8, bf16[32,512]{1,0:T(8,128)(2,1)S(1)} %copy-done.19, bf16[256,512]{1,0:T(8,128)(2,1)S(1)} %copy-done.12, ...), custom_call_target="tpu_custom_call" | custom-call | bytes 4472832 | tf_op jit(solution)/shard_map/pallas_call | solution.py:328
  57.0 2.1 %shard_map.123.mid_ref = bf16[256,2048]{1,0:T(8,128)(2,1)S(1)} custom-call(bf16[64,512]{1,0:T(8,128)(2,1)S(1)} %collective-permute-done.4.low_ref, bf16[256,512]{1,0:T(8,128)(2,1)S(1)} %get-tuple-element.17.grad_ref.mid_ref, bf16[64,512]{1,0:T(8,128)(2,1)S(1)} %collective-permute-done.5.high_ref, bf16[128,3456]{1,0:T(8,128)(2,1)S(1)} %copy-done, ...), custom_call_target="tpu_custom_call" | custom-call | bytes 9109504 | tf_op jit(solution)/shard_map/pallas_call | solution.py:328
  59.1 4.4 %collective-permute-start.6 = (bf16[32,2048]{1,0:T(8,128)(2,1)S(1)}, bf16[32,2048]{1,0:T(8,128)(2,1)S(1)}, u32[]{:S(2)}, u32[]{:S(2)}) collective-permute-start(bf16[32,2048]{1,0:T(8,128)(2,1)S(1)} %get-tuple-element.31), channel_id=1, source_target_pairs={{0,1},{1,2},{2,3},{3,4},{4,5},{5,6},{6,7},{7,8},{8,9},{9,10},{10,1... | collective-permute-start | bytes 393224 | tf_op jit(solution)/shard_map/ppermute | solution.py:366
  63.5 1.5 %collective-permute-start.7 = (bf16[32,2048]{1,0:T(8,128)(2,1)S(1)}, bf16[32,2048]{1,0:T(8,128)(2,1)S(1)}, u32[]{:S(2)}, u32[]{:S(2)}) collective-permute-start(bf16[32,2048]{1,0:T(8,128)(2,1)S(1)} %get-tuple-element.30), channel_id=1, source_target_pairs={{1,0},{2,1},{3,2},{4,3},{5,4},{6,5},{7,6},{8,7},{9,8},{10,9},{11,1... | collective-permute-start | bytes 393224 | tf_op jit(solution)/shard_map/ppermute | solution.py:367
  65.0 1.3 %copy_bitcast_fusion.3 = bf16[32,8,16,128]{3,2,1,0:T(8,128)(2,1)} fusion(bf16[8,32,16,128]{3,2,1,0:T(8,128)(2,1)S(1)} %bitcast.72), kind=kLoop, calls=%fused_computation.31 | loop fusion | bytes 2097152 | tf_op jit(solution)/shard_map/transpose | solution.py:359
  66.3 1.7 %collective-permute-done.7.high_ref = bf16[32,2048]{1,0:T(8,128)(2,1)S(1)} collective-permute-done((bf16[32,2048]{1,0:T(8,128)(2,1)S(1)}, bf16[32,2048]{1,0:T(8,128)(2,1)S(1)}, u32[]{:S(2)}, u32[]{:S(2)}) %collective-permute-start.7) | collective-permute-done | bytes 131104 | tf_op jit(solution)/shard_map/ppermute | solution.py:367
  68.0 7.1 %shard_map.124 = (f32[256,2048]{1,0:T(8,128)S(1)}, f32[288,96]{1,0:T(8,128)S(1)}) custom-call(bf16[32,2048]{1,0:T(8,128)(2,1)S(1)} %collective-permute-done.6.low_ref, bf16[256,2048]{1,0:T(8,128)(2,1)S(1)} %shard_map.123.mid_ref, bf16[32,2048]{1,0:T(8,128)(2,1)S(1)} %collective-permute-done.7.high_ref, bf16[128,1728]{1,0:T(8,128)(2,1)S(1)} %copy-done.3, ...), custom_call_target="tpu_custom_call" | custom-call | bytes 5603328 | tf_op jit(solution)/shard_map/pallas_call | solution.py:328
  75.1 22.0 %shard_map.125 = f32[768,128]{1,0:T(8,128)S(1)} custom-call(f32[288,96]{1,0:T(8,128)S(1)} %get-tuple-element.22.fine_ref, f32[864,64]{1,0:T(8,128)S(1)} %get-tuple-element.23.coarse_ref, f32[32,64]{1,0:T(8,128)S(1)} %get-tuple-element.24.up_ref), custom_call_target="tpu_custom_call" | custom-call | bytes 679936 | tf_op jit(solution)/shard_map/pallas_call | solution.py:328
  98.2 1.6 %copy_bitcast_fusion = f32[32,8,16,128]{3,2,1,0:T(8,128)} fusion(f32[8,32,16,128]{3,2,1,0:T(8,128)S(1)} %bitcast.71), kind=kLoop, calls=%fused_computation.8 | loop fusion | bytes 4194304 | tf_op jit(solution)/shard_map/transpose | solution.py:359
  (92 shorter events, 25.4 us)
Async XLA Ops:
  0.6 8.5 %copy-start.21 = (bf16[64,32,3,3,3]{0,1,4,3,2:T(8,128)(2,1)S(1)}, bf16[64,32,3,3,3]{0,1,4,3,2:T(8,128)(2,1)}, u32[]{:S(2)}) copy-start(bf16[64,32,3,3,3]{0,1,4,3,2:T(8,128)(2,1)} %param.11) | copy-start | bytes 331780
  2.4 12.0 %collective-permute-start = (bf16[32,2048]{1,0:T(8,128)(2,1)}, bf16[32,2048]{1,0:T(8,128)(2,1)S(1)}, u32[]{:S(2)}, u32[]{:S(2)}) collective-permute-start(bf16[32,2048]{1,0:T(8,128)(2,1)} %bitcast.60), channel_id=1, source_target_pairs={{0,1},{1,2},{2,3},{3,4},{4,5},{5,6},{6,7},{7,8},{8,9},{9,10},{10,1... | collective-permute-start | bytes 393224 | tf_op jit(solution)/shard_map/ppermute | solution.py:366
  5.4 9.0 %collective-permute-start.1 = (bf16[32,2048]{1,0:T(8,128)(2,1)}, bf16[32,2048]{1,0:T(8,128)(2,1)S(1)}, u32[]{:S(2)}, u32[]{:S(2)}) collective-permute-start(bf16[32,2048]{1,0:T(8,128)(2,1)} %bitcast.59), channel_id=1, source_target_pairs={{1,0},{2,1},{3,2},{4,3},{5,4},{6,5},{7,6},{8,7},{9,8},{10,9},{11,1... | collective-permute-start | bytes 393224 | tf_op jit(solution)/shard_map/ppermute | solution.py:367
  9.9 3.8 %copy-start.23 = (s32[1,2,16]{2,1,0:T(2,128)S(1)}, s32[1,2,16]{2,1,0:T(2,128)}, u32[]{:S(2)}) copy-start(s32[1,2,16]{2,1,0:T(2,128)} %param.9) | copy-start | bytes 388
  10.0 3.7 %copy-start.20 = (bf16[32,8,16,128]{3,2,1,0:T(8,128)(2,1)S(1)}, bf16[32,8,16,128]{3,2,1,0:T(8,128)(2,1)}, u32[]{:S(2)}) copy-start(bf16[32,8,16,128]{3,2,1,0:T(8,128)(2,1)} %param.8) | copy-start | bytes 3145732
  13.7 0.9 copy-start.10
  13.9 16.7 %copy-start.22 = (bf16[32,64]{1,0:T(8,128)(2,1)S(1)}, bf16[32,64]{1,0:T(8,128)(2,1)}, u32[]{:S(2)}) copy-start(bf16[32,64]{1,0:T(8,128)(2,1)} %param.12) | copy-start | bytes 12292
  20.5 1.3 %copy-start.1 = (f32[256,2048]{1,0:T(8,128)}, f32[256,2048]{1,0:T(8,128)S(1)}, u32[]{:S(2)}) copy-start(f32[256,2048]{1,0:T(8,128)S(1)} %get-tuple-element.20.slope_ref) | copy-start | bytes 6291460
  21.8 1.0 copy-start.4
  24.1 11.5 %collective-permute-start.2 = (bf16[32,512]{1,0:T(8,128)(2,1)}, bf16[32,512]{1,0:T(8,128)(2,1)S(1)}, u32[]{:S(2)}, u32[]{:S(2)}) collective-permute-start(bf16[32,512]{1,0:T(8,128)(2,1)} %get-tuple-element.39), channel_id=1, source_target_pairs={{0,1},{1,2},{2,3},{3,4},{4,5},{5,6},{6,7},{7,8},{8,9},{9,10},{10,1... | collective-permute-start | bytes 98312 | tf_op jit(solution)/shard_map/ppermute | solution.py:366
  29.3 6.9 %collective-permute-start.3 = (bf16[32,512]{1,0:T(8,128)(2,1)}, bf16[32,512]{1,0:T(8,128)(2,1)S(1)}, u32[]{:S(2)}, u32[]{:S(2)}) collective-permute-start(bf16[32,512]{1,0:T(8,128)(2,1)} %get-tuple-element.38), channel_id=1, source_target_pairs={{1,0},{2,1},{3,2},{4,3},{5,4},{6,5},{7,6},{8,7},{9,8},{10,9},{11,1... | collective-permute-start | bytes 98312 | tf_op jit(solution)/shard_map/ppermute | solution.py:367
  36.8 0.9 copy-start.7
  37.7 0.8 copy-start.13
  42.3 14.6 %collective-permute-start.4 = (bf16[64,512]{1,0:T(8,128)(2,1)S(1)}, bf16[64,512]{1,0:T(8,128)(2,1)S(1)}, u32[]{:S(2)}, u32[]{:S(2)}) collective-permute-start(bf16[64,512]{1,0:T(8,128)(2,1)S(1)} %get-tuple-element.37), channel_id=1, source_target_pairs={{0,1},{1,2},{2,3},{3,4},{4,5},{5,6},{6,7},{7,8},{8,9},{9,10},{10,1... | collective-permute-start | bytes 196616 | tf_op jit(solution)/shard_map/ppermute | solution.py:366
  46.6 10.3 %collective-permute-start.5 = (bf16[64,512]{1,0:T(8,128)(2,1)S(1)}, bf16[64,512]{1,0:T(8,128)(2,1)S(1)}, u32[]{:S(2)}, u32[]{:S(2)}) collective-permute-start(bf16[64,512]{1,0:T(8,128)(2,1)S(1)} %get-tuple-element.36), channel_id=1, source_target_pairs={{1,0},{2,1},{3,2},{4,3},{5,4},{6,5},{7,6},{8,7},{9,8},{10,9},{11,1... | collective-permute-start | bytes 196616 | tf_op jit(solution)/shard_map/ppermute | solution.py:367
  48.9 1.2 %copy-start.5 = (bf16[256,2048]{1,0:T(8,128)(2,1)S(1)}, bf16[256,2048]{1,0:T(8,128)(2,1)}, u32[]{:S(2)}) copy-start(bf16[256,2048]{1,0:T(8,128)(2,1)} %copy-done.4) | copy-start | bytes 3145732
  50.1 0.9 copy-start.8
  51.0 0.9 copy-start.9
  51.9 0.9 copy-start.12
  54.4 2.6 %copy-start = (bf16[128,3456]{1,0:T(8,128)(2,1)S(1)}, bf16[128,3456]{1,0:T(8,128)(2,1)}, u32[]{:S(2)}) copy-start(bf16[128,3456]{1,0:T(8,128)(2,1)} %fusion.22.taps_ref) | copy-start | bytes 2654212
  54.4 2.6 %copy-start.2 = (f32[256,2048]{1,0:T(8,128)S(1)}, f32[256,2048]{1,0:T(8,128)}, u32[]{:S(2)}) copy-start(f32[256,2048]{1,0:T(8,128)} %copy-done.1) | copy-start | bytes 6291460
  59.1 8.9 %copy-start.3 = (bf16[128,1728]{1,0:T(8,128)(2,1)S(1)}, bf16[128,1728]{1,0:T(8,128)(2,1)}, u32[]{:S(2)}) copy-start(bf16[128,1728]{1,0:T(8,128)(2,1)} %fusion.33.taps_ref) | copy-start | bytes 1327108
  59.1 7.2 %collective-permute-start.6 = (bf16[32,2048]{1,0:T(8,128)(2,1)S(1)}, bf16[32,2048]{1,0:T(8,128)(2,1)S(1)}, u32[]{:S(2)}, u32[]{:S(2)}) collective-permute-start(bf16[32,2048]{1,0:T(8,128)(2,1)S(1)} %get-tuple-element.31), channel_id=1, source_target_pairs={{0,1},{1,2},{2,3},{3,4},{4,5},{5,6},{6,7},{7,8},{8,9},{9,10},{10,1... | collective-permute-start | bytes 393224 | tf_op jit(solution)/shard_map/ppermute | solution.py:366
  63.5 4.5 %collective-permute-start.7 = (bf16[32,2048]{1,0:T(8,128)(2,1)S(1)}, bf16[32,2048]{1,0:T(8,128)(2,1)S(1)}, u32[]{:S(2)}, u32[]{:S(2)}) collective-permute-start(bf16[32,2048]{1,0:T(8,128)(2,1)S(1)} %get-tuple-element.30), channel_id=1, source_target_pairs={{1,0},{2,1},{3,2},{4,3},{5,4},{6,5},{7,6},{8,7},{9,8},{10,9},{11,1... | collective-permute-start | bytes 393224 | tf_op jit(solution)/shard_map/ppermute | solution.py:367
  (8 other events, 5.6 us)

commit v2 on v0

v2 whole, which is shorter than its diff:
```python
import functools
import math

import jax
import jax.numpy as jnp
import numpy as np
from jax import lax
from jax.experimental import pallas as pl
from jax.experimental.pallas import tpu as pltpu
from jax.sharding import PartitionSpec as P

F32 = jnp.float32
BF16 = jnp.bfloat16
VMEM_LIMIT = 48 * 1024 * 1024
MESH = pl.DeviceIdType.MESH
ALONG = 4


def dot(a, b):
    return jnp.dot(a, b, preferred_element_type=F32)


def dot_nt(a, b):
    return lax.dot_general(a, b, (((1,), (1,)), ((), ())), preferred_element_type=F32)


def dot_tn(a, b):
    return lax.dot_general(a, b, (((0,), (0,)), ((), ())), preferred_element_type=F32)


def halves(value):
    high = value.astype(BF16)
    return high, (value - high.astype(F32)).astype(BF16)


def pool_matrix(size_y):
    cell = np.arange(4 * size_y)
    coarse = np.arange(size_y)
    same_z = (cell // size_y // 2)[:, None] == (coarse // (size_y // 2))[None]
    same_y = (cell % size_y // 2)[:, None] == (coarse % (size_y // 2))[None]
    return (same_z & same_y).astype(np.float32)


def gather_fine(value, size_y, cols_ref, row, reverse):
    chans, length = value.shape
    wide = value.astype(F32)
    spot = lax.broadcasted_iota(jnp.int32, (chans, length), 1) % size_y
    before = jnp.where(spot == 0, 0.0, pltpu.roll(wide, 1, 1)).astype(BF16)
    after = jnp.where(spot == size_y - 1, 0.0, pltpu.roll(wide, length - 1, 1)).astype(BF16)
    edge = jnp.zeros((chans, size_y), BF16)
    blocks = (after, value, before) if reverse else (before, value, after)
    for k, shifted in enumerate(blocks):
        low = pl.ds(row + (k + (6 if reverse else 0)) * chans, chans)
        mid = pl.ds(row + (3 + k) * chans, chans)
        high = pl.ds(row + (k + (0 if reverse else 6)) * chans, chans)
        cols_ref[low, :size_y] = edge
        cols_ref[low, size_y:] = shifted[:, :-size_y]
        cols_ref[mid, :] = shifted
        cols_ref[high, : length - size_y] = shifted[:, size_y:]
        cols_ref[high, length - size_y :] = edge


def gather_coarse(value, size_y, cols_ref, row, reverse):
    chans, length = value.shape
    wide = value.astype(F32)
    cell = lax.broadcasted_iota(jnp.int32, (chans, length), 1)
    spot = cell % size_y
    for j in range(3):
        for k in range(3):
            shift = (j - 1) * size_y + (k - 1)
            rolled = pltpu.roll(wide, (-shift) % length, 1) if shift else wide
            if k == 0:
                rolled = jnp.where(spot == 0, 0.0, rolled)
            if k == 2:
                rolled = jnp.where(spot == size_y - 1, 0.0, rolled)
            if j == 0:
                rolled = jnp.where(cell < size_y, 0.0, rolled)
            if j == 2:
                rolled = jnp.where(cell >= length - size_y, 0.0, rolled)
            tap = 3 * j + k
            block = 8 - tap if reverse else tap
            cols_ref[pl.ds(row + block * chans, chans), :] = rolled.astype(BF16)


def gather_inner(gather, mid_ref, chans, size_y, cols_ref, reverse):
    depth = 9 * chans

    def body(plane, carry):
        start = pl.multiple_of(plane * chans, chans)
        row = pl.multiple_of((plane + 1) * depth, depth)
        gather(mid_ref[pl.ds(start, chans), :], size_y, cols_ref, row, reverse)
        return carry

    lax.fori_loop(0, mid_ref.shape[0] // chans, body, 0)


def gather_edges(gather, edge_ref, size_y, cols_ref, reverse):
    last = cols_ref.shape[0] - 9 * edge_ref.shape[1]
    gather(edge_ref[0], size_y, cols_ref, 0, reverse)
    gather(edge_ref[1], size_y, cols_ref, last, reverse)


def sum_pairs(value, chans):
    count = value.shape[0] // chans
    return jnp.concatenate(
        [
            value[(2 * i) * chans : (2 * i + 1) * chans]
            + value[(2 * i + 1) * chans : (2 * i + 2) * chans]
            for i in range(count // 2)
        ],
        axis=0,
    )


def repeat_pairs(value, chans):
    count = value.shape[0] // chans
    parts = [value[i // 2 * chans : (i // 2 + 1) * chans] for i in range(2 * count)]
    return jnp.concatenate(parts, axis=0)


def sigmoid(value):
    return 1.0 / (1.0 + jnp.exp(-value))


def whole_step(
    count, chunk, factor, size_y,
    rows_ref, cotangent_ref, fine_mask_ref, coarse_mask_ref, pool_ref, spread_ref,
    fine_taps_ref, coarse_taps_ref, coarse_back_ref, fine_back_ref, up_ref,
    net_ref, grad_rows_ref, grad_fine_ref, grad_coarse_ref, grad_up_ref,
    fine_cols, coarse_cols, inner_cols, hidden_ref, slope_ref, pooled_ref, inner_ref, grad_inner_ref,
    grad_pre_ref, lift_ref, framed, fine_edge, pooled_edge, inner_edge, grad_edge,
    packed, slots, part, whole,
    send_low, recv_low, send_high, recv_high, send_a, recv_a, send_b, recv_b,
):
    me = lax.axis_index("gx")
    out_chans, inner = up_ref.shape
    chans = out_chans
    planes = rows_ref.shape[0] // chans
    half = planes // 2
    length = rows_ref.shape[1]
    depth = 9 * chans
    wide = 4 * size_y
    steps = length // wide
    half_y = size_y // 2
    barrier = pltpu.get_barrier_semaphore()

    def peer(d):
        return lax.rem(me + d, count)

    def greet(d, carry):
        pl.semaphore_signal(barrier, inc=1, device_id={"gx": peer(d)}, device_id_type=MESH)
        return carry

    lax.fori_loop(1, count, greet, 0)

    def upward(index, values_ref, edge_ref):
        size = edge_ref.shape[1]
        return pltpu.make_async_remote_copy(
            src_ref=values_ref.at[pl.ds(values_ref.shape[0] - size, size)],
            dst_ref=edge_ref.at[0],
            send_sem=send_low.at[index],
            recv_sem=recv_low.at[index],
            device_id={"gx": lax.rem(me + 1, count)},
            device_id_type=MESH,
        )

    def downward(index, values_ref, edge_ref):
        size = edge_ref.shape[1]
        return pltpu.make_async_remote_copy(
            src_ref=values_ref.at[pl.ds(0, size)],
            dst_ref=edge_ref.at[1],
            send_sem=send_high.at[index],
            recv_sem=recv_high.at[index],
            device_id={"gx": lax.rem(me + count - 1, count)},
            device_id_type=MESH,
        )

    def start_upward(*args):
        @pl.when(me < count - 1)
        def _():
            upward(*args).start()

    def start_downward(*args):
        @pl.when(me > 0)
        def _():
            downward(*args).start()

    def finish_edges(*args):
        edge_ref = args[2]

        @pl.when(me > 0)
        def _():
            upward(*args).wait_recv()
            downward(*args).wait_send()

        @pl.when(me == 0)
        def _():
            edge_ref[0] = jnp.zeros(edge_ref.shape[1:], BF16)

        @pl.when(me < count - 1)
        def _():
            downward(*args).wait_recv()
            upward(*args).wait_send()

        @pl.when(me == count - 1)
        def _():
            edge_ref[1] = jnp.zeros(edge_ref.shape[1:], BF16)

    for step in range(steps):
        lanes = slice(step * wide, (step + 1) * wide)
        value = (cotangent_ref[:, lanes].astype(F32) * fine_mask_ref[:, lanes]).astype(BF16)
        lift_ref[:, step * size_y : (step + 1) * size_y] = sum_pairs(
            dot(value, pool_ref[...]), chans
        )
    empty = jnp.zeros((2 * chans, length), BF16)
    framed[: 2 * chans, :] = empty
    framed[2 * chans : (planes + 2) * chans, :] = rows_ref[...]
    framed[(planes + 2) * chans :, :] = empty

    pl.semaphore_wait(barrier, count - 1)
    start_upward(0, rows_ref, fine_edge)
    start_downward(0, rows_ref, fine_edge)
    gather_inner(gather_fine, rows_ref, chans, size_y, fine_cols, False)
    finish_edges(0, rows_ref, fine_edge)
    gather_edges(gather_fine, fine_edge, size_y, fine_cols, False)
    for group in range(planes // ALONG):
        rows = slice(group * ALONG * depth, (group * ALONG + ALONG + 2) * depth)
        held = slice(group * ALONG * chans, (group + 1) * ALONG * chans)
        out = slice(group * ALONG // 2 * chans, (group + 1) * ALONG // 2 * chans)
        for step in range(steps):
            lanes = slice(step * wide, (step + 1) * wide)
            pre = dot(fine_taps_ref[...], fine_cols[rows, lanes])
            mask = fine_mask_ref[:, lanes]
            sigma = sigmoid(pre)
            hidden = (pre * sigma * mask).astype(BF16)
            hidden_ref[held, lanes] = hidden
            slope_ref[held, lanes] = sigma * (1.0 + pre * (1.0 - sigma)) * mask
            pooled = sum_pairs(dot(hidden, pool_ref[...]), chans) * 0.125
            pooled_ref[out, step * size_y : (step + 1) * size_y] = pooled.astype(BF16)
        if group == 0:
            start_downward(1, pooled_ref, pooled_edge)
    start_upward(1, pooled_ref, pooled_edge)

    gather_inner(gather_coarse, pooled_ref, chans, half_y, coarse_cols, False)
    lift_high, lift_low = halves(lift_ref[...])
    up = up_ref[...]
    lifted_grads = []
    for x in range(half):
        held = slice(x * chans, (x + 1) * chans)
        lifted_grads.append(dot_tn(up, lift_high[held]) + dot_tn(up, lift_low[held]))
    grad_hidden = jnp.concatenate(lifted_grads, axis=0)
    finish_edges(1, pooled_ref, pooled_edge)
    gather_edges(gather_coarse, pooled_edge, half_y, coarse_cols, False)
    pre = dot(coarse_taps_ref[...], coarse_cols[...])
    mask = coarse_mask_ref[...]
    sigma = sigmoid(pre)
    slope = sigma * (1.0 + pre * (1.0 - sigma))
    grad_inner_ref[...] = (grad_hidden * mask * slope).astype(BF16)
    start_downward(2, grad_inner_ref, inner_edge)
    start_upward(2, grad_inner_ref, inner_edge)
    inner_ref[...] = (pre * sigma * mask).astype(BF16)
    gather_inner(gather_coarse, grad_inner_ref, inner, half_y, inner_cols, True)

    lifted = jnp.concatenate(
        [dot(up, inner_ref[x * inner : (x + 1) * inner, :]) for x in range(half)], axis=0
    )
    high, low = halves(lifted)
    for step in range(steps):
        lanes = slice(step * wide, (step + 1) * wide)
        coarse = slice(step * size_y, (step + 1) * size_y)
        spread = dot(high[:, coarse], spread_ref[...]) + dot(low[:, coarse], spread_ref[...])
        value = hidden_ref[:, lanes].astype(F32) + fine_mask_ref[:, lanes] * repeat_pairs(
            spread, chans
        )
        net_ref[:, lanes] = value.astype(BF16)
    grad_coarse = 0.0
    grad_up = 0.0
    for x in range(half):
        hidden = inner_ref[x * inner : (x + 1) * inner, :]
        held = slice(x * chans, (x + 1) * chans)
        grad_up += dot_nt(lift_high[held], hidden) + dot_nt(lift_low[held], hidden)
        grad_coarse += dot_nt(
            coarse_cols[x * depth : (x + 3) * depth, :],
            grad_inner_ref[x * inner : (x + 1) * inner, :],
        )
    split = 3 * depth // 2
    packed[depth + split + chans :, :] = jnp.zeros(
        (packed.shape[0] - depth - split - chans, packed.shape[1]), BF16
    )
    packed[depth : depth + split, :] = jnp.concatenate(
        [grad_coarse[:split], grad_coarse[split:]], axis=1
    ).astype(BF16)
    packed[depth + split : depth + split + chans, :] = jnp.concatenate(
        [grad_up, jnp.zeros_like(grad_up)], axis=1
    ).astype(BF16)

    finish_edges(2, grad_inner_ref, inner_edge)
    gather_edges(gather_coarse, inner_edge, half_y, inner_cols, True)
    high, low = halves(dot(coarse_back_ref[...], inner_cols[...]) * 0.125)
    for step in range(steps):
        lanes = slice(step * wide, (step + 1) * wide)
        coarse = slice(step * size_y, (step + 1) * size_y)
        spread = dot(high[:, coarse], spread_ref[...]) + dot(low[:, coarse], spread_ref[...])
        value = cotangent_ref[:, lanes].astype(F32) + repeat_pairs(spread, chans)
        grad_pre_ref[:, lanes] = (value * slope_ref[:, lanes]).astype(BF16)
    start_downward(3, grad_pre_ref, grad_edge)
    start_upward(3, grad_pre_ref, grad_edge)

    gather_inner(gather_fine, grad_pre_ref, chans, size_y, fine_cols, True)

    def taps_of(plane):
        return dot_nt(
            fine_cols[plane * depth : (plane + 1) * depth, :],
            framed[plane * chans : (plane + 3) * chans, :],
        )

    grad_fine = 0.0
    for plane in range(1, planes + 1):
        grad_fine += taps_of(plane)
    finish_edges(3, grad_pre_ref, grad_edge)
    gather_edges(gather_fine, grad_edge, size_y, fine_cols, True)
    grad_fine += taps_of(0) + taps_of(planes + 1)
    fill = packed.shape[1] - grad_fine.shape[1]
    packed[:depth, :] = jnp.concatenate(
        [grad_fine, jnp.zeros((depth, fill), F32)], axis=1
    ).astype(BF16)

    def rows_of(index):
        return pl.ds(pl.multiple_of(index * chunk, chunk), chunk)

    def scatter(d):
        return pltpu.make_async_remote_copy(
            src_ref=packed.at[rows_of(peer(d))],
            dst_ref=slots.at[d],
            send_sem=send_a.at[d],
            recv_sem=recv_a.at[d],
            device_id={"gx": peer(d)},
            device_id_type=MESH,
        )

    def collect(d):
        return pltpu.make_async_remote_copy(
            src_ref=part,
            dst_ref=whole.at[rows_of(me)],
            send_sem=send_b.at[d],
            recv_sem=recv_b.at[d],
            device_id={"gx": peer(d)},
            device_id_type=MESH,
        )

    def start(copy):
        def body(d, carry):
            copy(d).start()
            return carry

        lax.fori_loop(1, count, body, 0)

    def features_grad(group):
        rows = slice(group * ALONG * depth, (group * ALONG + ALONG + 2) * depth)
        held = slice(group * ALONG * chans, (group + 1) * ALONG * chans)
        for step in range(steps):
            lanes = slice(step * wide, (step + 1) * wide)
            grad_rows_ref[held, lanes] = dot(fine_back_ref[...], fine_cols[rows, lanes])

    start(scatter)
    groups = planes // ALONG
    for group in range(groups // 2):
        features_grad(group)

    def add(d, total):
        scatter(d).wait_recv()
        return total + slots[d].astype(F32)

    total = lax.fori_loop(1, count, add, packed[rows_of(me), :].astype(F32))
    part[...] = (total * factor).astype(BF16)
    start(collect)
    whole[rows_of(me), :] = part[...]
    for group in range(groups // 2, groups):
        features_grad(group)

    def finish(d, carry):
        scatter(d).wait_send()
        collect(d).wait_send()
        collect(d).wait_recv()
        return carry

    lax.fori_loop(1, count, finish, 0)
    sums = whole[...].astype(F32)
    for i in range(3):
        grad_fine_ref[i * depth : (i + 1) * depth, :] = sums[:depth, i * chans : (i + 1) * chans]
    grad_coarse_ref[:split, :] = sums[depth : depth + split, :inner]
    grad_coarse_ref[split:, :] = sums[depth : depth + split, inner : 2 * inner]
    grad_up_ref[...] = sums[depth + split : depth + split + chans, :inner]


def banded(taps, reverse):
    outs, _, depth = taps.shape
    parts = [taps[:, i] for i in (range(2, -1, -1) if reverse else range(3))]
    flat = jnp.concatenate(parts, axis=1)
    return jnp.concatenate(
        [jnp.pad(flat, ((0, 0), (x * depth, (ALONG - 1 - x) * depth))) for x in range(ALONG)],
        axis=0,
    )


def forward_taps(weight):
    outs, ins = weight.shape[:2]
    return banded(weight.transpose(0, 2, 3, 4, 1).reshape(outs, 3, 9 * ins), False)


def backward_taps(weight):
    outs, ins = weight.shape[:2]
    return banded(weight.transpose(1, 2, 3, 4, 0).reshape(ins, 3, 9 * outs), True)


def planes_first(values):
    chans, size_x, size_z, size_y = values.shape
    return values.transpose(1, 0, 2, 3).reshape(size_x * chans, size_z * size_y)


def channels_first(values, chans, size_z, size_y):
    return values.reshape(-1, chans, size_z, size_y).transpose(1, 0, 2, 3)


def expand_row(blocks, times):
    values = blocks.astype(F32)[0]
    size_z, size_y = values.shape
    values = jnp.broadcast_to(values[:, None, :, None], (size_z, times, size_y, times))
    return values.reshape(1, size_z * times * size_y * times)


def per_device(features, active_blocks, weight_fine, weight_coarse, weight_up, cotangent):
    chans, size_x, size_z, size_y = features.shape
    inner = weight_coarse.shape[0]
    count = lax.axis_size("gx")
    factor = 1.0 / math.sqrt(size_x * count * size_z * size_y)
    length = size_z * size_y
    half_x, coarse_length = size_x // 2, length // 4
    used = 9 * chans + (27 * chans) // 2 + chans
    chunk = -(-used // (16 * count)) * 16
    lanes = 2 * inner
    shape = jax.ShapeDtypeStruct
    args = (
        planes_first(features),
        planes_first(cotangent),
        expand_row(active_blocks, 8),
        expand_row(active_blocks, 4),
        jnp.asarray(pool_matrix(size_y), BF16),
        jnp.asarray(pool_matrix(size_y).T, BF16),
        forward_taps(weight_fine),
        forward_taps(weight_coarse),
        backward_taps(weight_coarse),
        backward_taps(weight_fine),
        weight_up,
    )
    out_shape = (
        shape((size_x * chans, length), BF16),
        shape((size_x * chans, length), F32),
        shape((27 * chans, chans), F32),
        shape((27 * chans, inner), F32),
        shape((chans, inner), F32),
    )
    scratch = [
        pltpu.VMEM(((size_x + 2) * 9 * chans, length), BF16),
        pltpu.VMEM(((half_x + 2) * 9 * chans, coarse_length), BF16),
        pltpu.VMEM(((half_x + 2) * 9 * inner, coarse_length), BF16),
        pltpu.VMEM((size_x * chans, length), BF16),
        pltpu.VMEM((size_x * chans, length), F32),
        pltpu.VMEM((half_x * chans, coarse_length), BF16),
        pltpu.VMEM((half_x * inner, coarse_length), BF16),
        pltpu.VMEM((half_x * inner, coarse_length), BF16),
        pltpu.VMEM((size_x * chans, length), BF16),
        pltpu.VMEM((half_x * chans, coarse_length), F32),
        pltpu.VMEM(((size_x + 4) * chans, length), BF16),
        pltpu.VMEM((2, chans, length), BF16),
        pltpu.VMEM((2, chans, coarse_length), BF16),
        pltpu.VMEM((2, inner, coarse_length), BF16),
        pltpu.VMEM((2, chans, length), BF16),
        pltpu.VMEM((count * chunk, lanes), BF16),
        pltpu.VMEM((count, chunk, lanes), BF16),
        pltpu.VMEM((chunk, lanes), BF16),
        pltpu.VMEM((count * chunk, lanes), BF16),
    ]
    scratch += [pltpu.SemaphoreType.DMA((4,))] * 4 + [pltpu.SemaphoreType.DMA((count,))] * 4
    net_rows, grad_rows, grad_fine, grad_coarse, grad_up = pl.pallas_call(
        functools.partial(whole_step, count, chunk, factor, size_y),
        out_shape=out_shape,
        in_specs=[pl.BlockSpec(memory_space=pltpu.VMEM)] * len(args),
        out_specs=tuple(pl.BlockSpec(memory_space=pltpu.VMEM) for _ in out_shape),
        scratch_shapes=scratch,
        compiler_params=pltpu.CompilerParams(
            vmem_limit_bytes=VMEM_LIMIT, collective_id=0, has_side_effects=True
        ),
    )(*args)
    taps = (3, 3, 3)
    return (
        channels_first(net_rows, chans, size_z, size_y),
        channels_first(grad_rows, chans, size_z, size_y),
        grad_fine.reshape(taps + (chans, chans)).transpose(3, 4, 0, 1, 2),
        grad_coarse.reshape(taps + (chans, inner)).transpose(4, 3, 0, 1, 2),
        grad_up,
    )


def solution(mesh):
    return jax.shard_map(
        per_device,
        mesh=mesh,
        in_specs=(
            P(None, ("groups", "gx"), None, None),
            P(("groups", "gx"), None, None),
            P(),
            P(),
            P(),
            P(None, ("groups", "gx"), None, None),
        ),
        out_specs=(
            P(None, ("groups", "gx"), None, None),
            P(None, ("groups", "gx"), None, None),
            P("groups", None, None, None, None),
            P("groups", None, None, None, None),
            P("groups", None),
        ),
        check_vma=False,
    )
```

time: 398 us -> 59.4 us (0.15); the launches traced: 392 us -> 59.1 us
  local copies, waits for them, and re-layouts: 130 us -> 12.1 us
  waiting for transfers between devices: 70.7 us -> 0 us
  blocking collectives: 63.2 us -> 0 us
  matrix products: 60.6 us -> 0 us
  Pallas kernels: 0 us -> 44.6 us
  other arithmetic: 34.8 us -> 1.51 us
  starting transfers between devices: 17.9 us -> 0 us
  between operations: 15.1 us -> 0.88 us
    psum x1 -> x0, waiting for transfers between devices: 69.7 us -> none  [per_device(): lax.psum((grad_fine, grad_coarse, grad_up), 'gx')]
    psum x1 -> x0, blocking collectives: 63.2 us -> none  [per_device(): lax.psum((grad_fine, grad_coarse, grad_up), 'gx')]
    dot_general x69 -> x0, matrix products: 60.6 us -> none  [the longest x12 34.7 us: conv_rows(): jnp.einsum('oc,cxzy->oxzy', taps, stacked, preferred_element_type=jnp.flo...]
    pallas_call x0 -> x1, Pallas kernels: none -> 44.6 us  [per_device(): pl.pallas_call(functools.partial(whole_step, count, chunk, factor, size_y...]
    concatenate x8 -> x1, local copies, waits for them, and re-layouts: 42.7 us -> 0.1 us  [banded(): flat = jnp.concatenate(parts, axis=1)]
    unnamed x85 -> x27, local copies, waits for them, and re-layouts: 27.5 us -> 4.3 us
    reduce_sum x2 -> x0, other arithmetic: 18.4 us -> none  [pool_sum(): values.reshape(chans, size_x // 2, 2, size_z // 2, 2, size_y // 2, 2)]
    ppermute x8 -> x0, starting transfers between devices: 17.9 us -> none  [the longest x4 12.2 us: extended(): lax.ppermute(lax.slice_in_dim(block, block.shape[dim] - width, None, axis...]
  transfers between devices with their start and end apart: 9 -> 0, of which waited for: 2 -> 0; matrix products, arithmetic and copies ran while one was open for 20% -> 0% of each run, Pallas kernels for 0% -> 0%
where the time goes in v2:
time: 59.4 us; the launch traced here: 59.1 us
  Pallas kernels  44.6 us (75%)
  local copies, waits for them, and re-layouts  12.1 us (20%)
  other arithmetic  1.51 us (3%)
  between operations  0.88 us (1%)
    pallas_call x1, Pallas kernels, per_device(): pl.pallas_call(functools.partial(whole_step, count, chunk, factor, size_y...  44.6 us
    unnamed x27, local copies, waits for them, and re-layouts  4.3 us
    transpose x2, local copies, waits for them, and re-layouts, channels_first(): return values.reshape(-1, chans, size_z, size_y).transpose(1, 0, 2, 3)  2.83 us
    slice x2, local copies, waits for them, and re-layouts, banded(): parts = [taps[:, i] for i in (range(2, -1, -1) if reverse else range(3))]  1.95 us
    reshape x1, local copies, waits for them, and re-layouts, planes_first(): return values.transpose(1, 0, 2, 3).reshape(size_x * chans, size_z * size_y)  1.48 us

profile of v2, /device:TPU:0, one launch (start us, length us, event | category | flops | bytes accessed | tf_op | source)
XLA Modules:
  0.0 59.1 jit_solution(4982141304817890665)
XLA Ops:
  0.6 0.7 %convert_bitcast_fusion = f32[2,16]{1,0:T(2,128)S(1)} fusion(s32[1,2,16]{2,1,0:T(2,128)} %param.9), kind=kLoop, calls=%fused_computation.65 | loop fusion | flops 32 | bytes 256 | tf_op jit(solution)/shard_map/broadcast_in_dim | solution.py:428
  1.8 1.0 %fusion.35 = (bf16[64,1,288]{0,2,1:T(8,128)(2,1)S(1)}, bf16[64,1,288]{0,2,1:T(8,128)(2,1)S(1)}, bf16[64,1,288]{0,2,1:T(8,128)(2,1)S(1)}) fusion(bf16[64,3,288]{0,2,1:T(8,128)(2,1)} %bitcast.80), kind=kLoop, calls=%fused_computation.67 | loop fusion | bytes 221184 | tf_op jit(solution)/shard_map/slice | solution.py:398
  3.2 1.0 %fusion.34 = (bf16[32,1,288]{0,2,1:T(8,128)(2,1)S(1)}, bf16[32,1,288]{0,2,1:T(8,128)(2,1)S(1)}, bf16[32,1,288]{0,2,1:T(8,128)(2,1)S(1)}) fusion(bf16[32,3,288]{0,2,1:T(8,128)(2,1)} %bitcast.82), kind=kLoop, calls=%fused_computation.66 | loop fusion | bytes 110592 | tf_op jit(solution)/shard_map/slice | solution.py:398
  4.5 0.2 copy.27
  4.7 0.2 reshape.53
  5.1 0.2 copy.23
  5.2 0.2 reshape.51
  5.5 0.1 fusion.22.coarse_back_ref
  5.7 0.2 fusion.13.coarse_taps_ref
  5.9 0.2 fusion.30
  6.1 0.4 copy-done.4
  6.5 0.2 copy.21
  6.6 0.3 copy-done.5
  7.0 0.2 copy.22
  7.2 1.5 %copy_bitcast_fusion.1 = (bf16[256,2048]{1,0:T(8,128)(2,1)}, bf16[256,2048]{1,0:T(8,128)(2,1)S(1)}) fusion(bf16[32,8,16,128]{3,2,1,0:T(8,128)(2,1)S(1)} %bitcast.76, bf16[32,8,16,128]{3,2,1,0:T(8,128)(2,1)S(1)} %bitcast.75), kind=kLoop, calls=%fused_computation.29 | loop fusion | bytes 4194304 | tf_op jit(solution)/shard_map/reshape | solution.py:418
  8.7 44.6 %shard_map.119 = (bf16[256,2048]{1,0:T(8,128)(2,1)S(1)}, f32[256,2048]{1,0:T(8,128)}, f32[864,32]{1,0:T(8,128)S(1)}, f32[864,64]{1,0:T(8,128)S(1)}, f32[32,64]{1,0:T(8,128)S(1)}) custom-call(bf16[256,2048]{1,0:T(8,128)(2,1)S(1)} %get-tuple-element.28.rows_ref, bf16[256,2048]{1,0:T(8,128)(2,1)} %get-tuple-element.27.cotangent_ref, ...), custom_call_target="tpu_custom_call" | custom-call | tf_op jit(solution)/shard_map/pallas_call | solution.py:485
  53.3 0.2 copy.40
  53.5 1.3 %copy_bitcast_fusion.3 = bf16[32,8,16,128]{3,2,1,0:T(8,128)(2,1)} fusion(bf16[8,32,16,128]{3,2,1,0:T(8,128)(2,1)S(1)} %bitcast.74), kind=kLoop, calls=%fused_computation.31 | loop fusion | bytes 2097152 | tf_op jit(solution)/shard_map/transpose | solution.py:422
  54.8 0.2 copy-done.3
  55.0 0.4 copy.41
  55.4 1.6 %copy_bitcast_fusion = f32[32,8,16,128]{3,2,1,0:T(8,128)} fusion(f32[8,32,16,128]{3,2,1,0:T(8,128)S(1)} %bitcast.73), kind=kLoop, calls=%fused_computation.8 | loop fusion | bytes 4194304 | tf_op jit(solution)/shard_map/transpose | solution.py:422
  57.0 0.8 %copy.49 = f32[32,32,3,3,3]{1,0,4,3,2:T(8,128)} copy(f32[32,32,3,3,3]{1,0,4,3,2:T(8,128)S(1)} %bitcast.72) | data formatting | bytes 221184
  57.7 0.8 %copy.50 = f32[64,32,3,3,3]{0,1,4,3,2:T(8,128)} copy(f32[64,32,3,3,3]{0,1,4,3,2:T(8,128)S(1)} %bitcast.71) | data formatting | bytes 442368
  58.5 0.6 %copy.51 = f32[32,64]{1,0:T(8,128)} copy(f32[32,64]{1,0:T(8,128)S(1)} %get-tuple-element.40) | data formatting | bytes 16384
  (29 shorter events, 1.4 us)
Async XLA Ops:
  0.6 3.9 %copy-start.6 = (bf16[64,32,3,3,3]{0,1,4,3,2:T(8,128)(2,1)S(1)}, bf16[64,32,3,3,3]{0,1,4,3,2:T(8,128)(2,1)}, u32[]{:S(2)}) copy-start(bf16[64,32,3,3,3]{0,1,4,3,2:T(8,128)(2,1)} %param.11) | copy-start | bytes 331780
  1.5 3.5 %copy-start.7 = (bf16[32,32,3,3,3]{1,0,4,3,2:T(8,128)(2,1)S(1)}, bf16[32,32,3,3,3]{1,0,4,3,2:T(8,128)(2,1)}, u32[]{:S(2)}) copy-start(bf16[32,32,3,3,3]{1,0,4,3,2:T(8,128)(2,1)} %param.10) | copy-start | bytes 165892
  5.2 1.2 %copy-start.4 = (bf16[32,8,16,128]{3,2,1,0:T(8,128)(2,1)S(1)}, bf16[32,8,16,128]{3,2,1,0:T(8,128)(2,1)}, u32[]{:S(2)}) copy-start(bf16[32,8,16,128]{3,2,1,0:T(8,128)(2,1)} %param.8) | copy-start | bytes 3145732
  5.7 1.3 %copy-start.5 = (bf16[32,8,16,128]{3,2,1,0:T(8,128)(2,1)S(1)}, bf16[32,8,16,128]{3,2,1,0:T(8,128)(2,1)}, u32[]{:S(2)}) copy-start(bf16[32,8,16,128]{3,2,1,0:T(8,128)(2,1)} %param.13) | copy-start | bytes 3145732
  7.2 1.5 %copy-start = (bf16[128,512]{1,0:T(8,128)(2,1)S(1)}, bf16[128,512]{1,0:T(8,128)(2,1)}, u32[]{:S(2)}) copy-start(bf16[128,512]{1,0:T(8,128)(2,1)} %constant.8.clone.spread_ref) | copy-start | bytes 393220
  7.2 1.5 %copy-start.1 = (bf16[512,128]{1,0:T(8,128)(2,1)S(1)}, bf16[512,128]{1,0:T(8,128)(2,1)}, u32[]{:S(2)}) copy-start(bf16[512,128]{1,0:T(8,128)(2,1)} %constant.7.clone.pool_ref) | copy-start | bytes 393220
  7.2 1.5 %copy-start.2 = (bf16[32,64]{1,0:T(8,128)(2,1)S(1)}, bf16[32,64]{1,0:T(8,128)(2,1)}, u32[]{:S(2)}) copy-start(bf16[32,64]{1,0:T(8,128)(2,1)} %up_ref.1) | copy-start | bytes 12292
  53.3 1.8 %copy-start.3 = (f32[256,2048]{1,0:T(8,128)S(1)}, f32[256,2048]{1,0:T(8,128)}, u32[]{:S(2)}) copy-start(f32[256,2048]{1,0:T(8,128)} %get-tuple-element.11) | copy-start | bytes 6291460

commit v3 on v2

--- a/solution.py
+++ b/solution.py
@@ -123,14 +123,14 @@
 
 
 def whole_step(
-    count, chunk, factor, size_y,
+    count, factor, size_y,
     rows_ref, cotangent_ref, fine_mask_ref, coarse_mask_ref, pool_ref, spread_ref,
     fine_taps_ref, coarse_taps_ref, coarse_back_ref, fine_back_ref, up_ref,
     net_ref, grad_rows_ref, grad_fine_ref, grad_coarse_ref, grad_up_ref,
     fine_cols, coarse_cols, inner_cols, hidden_ref, slope_ref, pooled_ref, inner_ref, grad_inner_ref,
     grad_pre_ref, lift_ref, framed, fine_edge, pooled_edge, inner_edge, grad_edge,
-    packed, slots, part, whole,
-    send_low, recv_low, send_high, recv_high, send_a, recv_a, send_b, recv_b,
+    inner_sum, fine_sum,
+    send_low, recv_low, send_high, recv_high,
 ):
     me = lax.axis_index("gx")
     out_chans, inner = up_ref.shape
@@ -152,6 +152,61 @@
         return carry
 
     lax.fori_loop(1, count, greet, 0)
+
+    def scatter(refs, d):
+        packed, slots, _, _, send, recv, _, _ = refs
+        chunk = slots.shape[1]
+        return pltpu.make_async_remote_copy(
+            src_ref=packed.at[pl.ds(pl.multiple_of(peer(d) * chunk, chunk), chunk)],
+            dst_ref=slots.at[d],
+            send_sem=send.at[d],
+            recv_sem=recv.at[d],
+            device_id={"gx": peer(d)},
+            device_id_type=MESH,
+        )
+
+    def collect(refs, d):
+        _, _, part, whole, _, _, send, recv = refs
+        chunk = part.shape[0]
+        return pltpu.make_async_remote_copy(
+            src_ref=part,
+            dst_ref=whole.at[pl.ds(pl.multiple_of(me * chunk, chunk), chunk)],
+            send_sem=send.at[d],
+            recv_sem=recv.at[d],
+            device_id={"gx": peer(d)},
+            device_id_type=MESH,
+        )
+
+    def start(copy, refs):
+        def body(d, carry):
+            copy(refs, d).start()
+            return carry
+
+        lax.fori_loop(1, count, body, 0)
+
+    def add_up(refs):
+        packed, slots, part, whole = refs[:4]
+        chunk = part.shape[0]
+        mine = pl.ds(pl.multiple_of(me * chunk, chunk), chunk)
+
+        def add(d, total):
+            scatter(refs, d).wait_recv()
+            return total + slots[d].astype(F32)
+
+        total = lax.fori_loop(1, count, add, packed[mine, :].astype(F32))
+        part[...] = (total * factor).astype(BF16)
+        start(collect, refs)
+        whole[mine, :] = part[...]
+
+    def finish(refs):
+        def body(d, carry):
+            scatter(refs, d).wait_send()
+            collect(refs, d).wait_send()
+            collect(refs, d).wait_recv()
+            return carry
+
+        lax.fori_loop(1, count, body, 0)
+        return refs[3][...].astype(F32)
 
     def upward(index, values_ref, edge_ref):
         size = edge_ref.shape[1]
@@ -284,15 +339,17 @@
             grad_inner_ref[x * inner : (x + 1) * inner, :],
         )
     split = 3 * depth // 2
-    packed[depth + split + chans :, :] = jnp.zeros(
-        (packed.shape[0] - depth - split - chans, packed.shape[1]), BF16
-    )
-    packed[depth : depth + split, :] = jnp.concatenate(
-        [grad_coarse[:split], grad_coarse[split:]], axis=1
+    packed = inner_sum[0]
+    fill = packed.shape[0] - split - chans
+    packed[...] = jnp.concatenate(
+        [
+            jnp.concatenate([grad_coarse[:split], grad_coarse[split:]], axis=1),
+            jnp.concatenate([grad_up, jnp.zeros_like(grad_up)], axis=1),
+            jnp.zeros((fill, 2 * inner), F32),
+        ],
+        axis=0,
     ).astype(BF16)
-    packed[depth + split : depth + split + chans, :] = jnp.concatenate(
-        [grad_up, jnp.zeros_like(grad_up)], axis=1
-    ).astype(BF16)
+    start(scatter, inner_sum)
 
     finish_edges(2, grad_inner_ref, inner_edge)
     gather_edges(gather_coarse, inner_edge, half_y, inner_cols, True)
@@ -307,6 +364,7 @@
     start_upward(3, grad_pre_ref, grad_edge)
 
     gather_inner(gather_fine, grad_pre_ref, chans, size_y, fine_cols, True)
+    add_up(inner_sum)
 
     def taps_of(plane):
         return dot_nt(
@@ -320,40 +378,19 @@
     finish_edges(3, grad_pre_ref, grad_edge)
     gather_edges(gather_fine, grad_edge, size_y, fine_cols, True)
     grad_fine += taps_of(0) + taps_of(planes + 1)
-    fill = packed.shape[1] - grad_fine.shape[1]
-    packed[:depth, :] = jnp.concatenate(
-        [grad_fine, jnp.zeros((depth, fill), F32)], axis=1
+    tall = 3 * depth // 4
+    short = depth - tall
+    packed = fine_sum[0]
+    rest = jnp.concatenate(
+        [grad_fine[tall:, i * chans : (i + 1) * chans] for i in range(3)], axis=0
+    )
+    packed[...] = jnp.concatenate(
+        [
+            jnp.concatenate([grad_fine[:tall], rest], axis=1),
+            jnp.zeros((packed.shape[0] - tall, 4 * chans), F32),
+        ],
+        axis=0,
     ).astype(BF16)
-
-    def rows_of(index):
-        return pl.ds(pl.multiple_of(index * chunk, chunk), chunk)
-
-    def scatter(d):
-        return pltpu.make_async_remote_copy(
-            src_ref=packed.at[rows_of(peer(d))],
-            dst_ref=slots.at[d],
-            send_sem=send_a.at[d],
-            recv_sem=recv_a.at[d],
-            device_id={"gx": peer(d)},
-            device_id_type=MESH,
-        )
-
-    def collect(d):
-        return pltpu.make_async_remote_copy(
-            src_ref=part,
-            dst_ref=whole.at[rows_of(me)],
-            send_sem=send_b.at[d],
-            recv_sem=recv_b.at[d],
-            device_id={"gx": peer(d)},
-            device_id_type=MESH,
-        )
-
-    def start(copy):
-        def body(d, carry):
-            copy(d).start()
-            return carry
-
-        lax.fori_loop(1, count, body, 0)
 
     def features_grad(group):
         rows = slice(group * ALONG * depth, (group * ALONG + ALONG + 2) * depth)
@@ -362,41 +399,28 @@
             lanes = slice(step * wide, (step + 1) * wide)
             grad_rows_ref[held, lanes] = dot(fine_back_ref[...], fine_cols[rows, lanes])
 
-    start(scatter)
+    start(scatter, fine_sum)
     groups = planes // ALONG
     for group in range(groups // 2):
         features_grad(group)
-
-    def add(d, total):
-        scatter(d).wait_recv()
-        return total + slots[d].astype(F32)
-
-    total = lax.fori_loop(1, count, add, packed[rows_of(me), :].astype(F32))
-    part[...] = (total * factor).astype(BF16)
-    start(collect)
-    whole[rows_of(me), :] = part[...]
+    add_up(fine_sum)
     for group in range(groups // 2, groups):
         features_grad(group)
-
-    def finish(d, carry):
-        scatter(d).wait_send()
-        collect(d).wait_send()
-        collect(d).wait_recv()
-        return carry
-
-    lax.fori_loop(1, count, finish, 0)
-    sums = whole[...].astype(F32)
+    sums = finish(inner_sum)
+    grad_coarse_ref[:split, :] = sums[:split, :inner]
+    grad_coarse_ref[split:, :] = sums[:split, inner : 2 * inner]
+    grad_up_ref[...] = sums[split : split + chans, :inner]
+    sums = finish(fine_sum)
     for i in range(3):
-        grad_fine_ref[i * depth : (i + 1) * depth, :] = sums[:depth, i * chans : (i + 1) * chans]
-    grad_coarse_ref[:split, :] = sums[depth : depth + split, :inner]
-    grad_coarse_ref[split:, :] = sums[depth : depth + split, inner : 2 * inner]
-    grad_up_ref[...] = sums[depth + split : depth + split + chans, :inner]
-
-
-def banded(taps, reverse):
-    outs, _, depth = taps.shape
-    parts = [taps[:, i] for i in (range(2, -1, -1) if reverse else range(3))]
-    flat = jnp.concatenate(parts, axis=1)
+        row = i * depth
+        grad_fine_ref[row : row + tall, :] = sums[:tall, i * chans : (i + 1) * chans]
+        grad_fine_ref[row + tall : row + depth, :] = sums[
+            i * short : (i + 1) * short, 3 * chans : 4 * chans
+        ]
+
+
+def banded(flat):
+    depth = flat.shape[1] // 3
     return jnp.concatenate(
         [jnp.pad(flat, ((0, 0), (x * depth, (ALONG - 1 - x) * depth))) for x in range(ALONG)],
         axis=0,
@@ -405,12 +429,13 @@
 
 def forward_taps(weight):
     outs, ins = weight.shape[:2]
-    return banded(weight.transpose(0, 2, 3, 4, 1).reshape(outs, 3, 9 * ins), False)
+    return banded(weight.transpose(0, 2, 3, 4, 1).reshape(outs, 27 * ins))
 
 
 def backward_taps(weight):
     outs, ins = weight.shape[:2]
-    return banded(weight.transpose(1, 2, 3, 4, 0).reshape(ins, 3, 9 * outs), True)
+    taps = weight.transpose(1, 2, 3, 4, 0).reshape(ins, 3, 9 * outs)
+    return banded(jnp.concatenate([taps[:, i] for i in (2, 1, 0)], axis=1))
 
 
 def planes_first(values):
@@ -436,9 +461,16 @@
     factor = 1.0 / math.sqrt(size_x * count * size_z * size_y)
     length = size_z * size_y
     half_x, coarse_length = size_x // 2, length // 4
-    used = 9 * chans + (27 * chans) // 2 + chans
-    chunk = -(-used // (16 * count)) * 16
-    lanes = 2 * inner
+
+    def sum_scratch(rows, lanes):
+        chunk = -(-rows // (16 * count)) * 16
+        return (
+            pltpu.VMEM((count * chunk, lanes), BF16),
+            pltpu.VMEM((count, chunk, lanes), BF16),
+            pltpu.VMEM((chunk, lanes), BF16),
+            pltpu.VMEM((count * chunk, lanes), BF16),
+        ) + (pltpu.SemaphoreType.DMA((count,)),) * 4
+
     shape = jax.ShapeDtypeStruct
     args = (
         planes_first(features),
@@ -476,14 +508,12 @@
         pltpu.VMEM((2, chans, coarse_length), BF16),
         pltpu.VMEM((2, inner, coarse_length), BF16),
         pltpu.VMEM((2, chans, length), BF16),
-        pltpu.VMEM((count * chunk, lanes), BF16),
-        pltpu.VMEM((count, chunk, lanes), BF16),
-        pltpu.VMEM((chunk, lanes), BF16),
-        pltpu.VMEM((count * chunk, lanes), BF16),
+        sum_scratch(27 * chans // 2 + chans, 2 * inner),
+        sum_scratch(27 * chans // 4, 4 * chans),
     ]
-    scratch += [pltpu.SemaphoreType.DMA((4,))] * 4 + [pltpu.SemaphoreType.DMA((count,))] * 4
+    scratch += [pltpu.SemaphoreType.DMA((4,))] * 4
     net_rows, grad_rows, grad_fine, grad_coarse, grad_up = pl.pallas_call(
-        functools.partial(whole_step, count, chunk, factor, size_y),
+        functools.partial(whole_step, count, factor, size_y),
         out_shape=out_shape,
         in_specs=[pl.BlockSpec(memory_space=pltpu.VMEM)] * len(args),
         out_specs=tuple(pl.BlockSpec(memory_space=pltpu.VMEM) for _ in out_shape),

time: 59.4 us -> 59.2 us (level)
  Pallas kernels: 44.6 us -> 43.8 us
  local copies, waits for them, and re-layouts: 12.1 us -> 12.9 us
    reshape x2 -> x3, local copies, waits for them, and re-layouts: 0.4 us -> 1.48 us  [the longest x2 1.26 us: forward_taps(): return banded(weight.transpose(0, 2, 3, 4, 1).reshape(outs, 27 * ins))]
    slice x2 -> x1, local copies, waits for them, and re-layouts: 1.95 us -> 0.98 us  [backward_taps(): return banded(jnp.concatenate([taps[:, i] for i in (2, 1, 0)], axis=1))]
    transpose x2, local copies, waits for them, and re-layouts: 0.31 us -> 1.25 us  [the longest x1 1.09 us: backward_taps(): taps = weight.transpose(1, 2, 3, 4, 0).reshape(ins, 3, 9 * outs)]
    pallas_call x1, Pallas kernels: 44.6 us -> 43.8 us  [per_device(): pl.pallas_call(functools.partial(whole_step, count, factor, size_y), out_...]
    unnamed x27 -> x22, local copies, waits for them, and re-layouts: 4.3 us -> 3.99 us
where the time goes in v3:
time: 59.2 us; the launch traced here: 58.8 us
  Pallas kernels  43.8 us (74%)
  local copies, waits for them, and re-layouts  12.9 us (22%)
  other arithmetic  1.32 us (2%)
  between operations  0.83 us (1%)
    pallas_call x1, Pallas kernels, per_device(): pl.pallas_call(functools.partial(whole_step, count, factor, size_y), out_...  43.8 us
    unnamed x22, local copies, waits for them, and re-layouts  3.99 us
    transpose x2, local copies, waits for them, and re-layouts, channels_first(): return values.reshape(-1, chans, size_z, size_y).transpose(1, 0, 2, 3)  2.83 us
    reshape x1, local copies, waits for them, and re-layouts, planes_first(): return values.transpose(1, 0, 2, 3).reshape(size_x * chans, size_z * size_y)  1.48 us
    reshape x2, local copies, waits for them, and re-layouts, forward_taps(): return banded(weight.transpose(0, 2, 3, 4, 1).reshape(outs, 27 * ins))  1.26 us

profile of v3, /device:TPU:0, one launch (start us, length us, event | category | flops | bytes accessed | tf_op | source)
XLA Modules:
  0.0 58.8 jit_solution(5919114107168906057)
XLA Ops:
  0.6 0.7 %convert_bitcast_fusion = f32[2,16]{1,0:T(2,128)S(1)} fusion(s32[1,2,16]{2,1,0:T(2,128)} %param.9), kind=kLoop, calls=%fused_computation.60 | loop fusion | flops 32 | bytes 256 | tf_op jit(solution)/shard_map/broadcast_in_dim | solution.py:453
  1.5 1.1 %copy.24 = bf16[64,864]{1,0:T(8,128)(2,1)S(1)} copy(bf16[64,864]{0,1:T(8,128)(2,1)} %bitcast.71) | data formatting | bytes 221184 | tf_op jit(solution)/shard_map/reshape | solution.py:432
  2.8 1.0 %fusion.34 = (bf16[32,1,288]{0,2,1:T(8,128)(2,1)S(1)}, bf16[32,1,288]{0,2,1:T(8,128)(2,1)S(1)}, bf16[32,1,288]{0,2,1:T(8,128)(2,1)S(1)}) fusion(bf16[32,3,288]{0,2,1:T(8,128)(2,1)} %bitcast.69), kind=kLoop, calls=%fused_computation.61 | loop fusion | bytes 110592 | tf_op jit(solution)/shard_map/slice | solution.py:438
  4.2 1.1 %copy.28 = bf16[32,3,3,3,64]{4,3,2,0,1:T(4,128)(2,1)S(1)} copy(bf16[32,3,3,3,64]{4,0,3,2,1:T(8,128)(2,1)} %bitcast.72) | data formatting | bytes 221184 | tf_op jit(solution)/shard_map/transpose | solution.py:437
  5.3 0.2 reshape.53
  5.6 0.2 copy.23
  5.8 0.2 reshape.51
  6.0 0.1 fusion.22.coarse_back_ref
  6.2 0.2 fusion.13.coarse_taps_ref
  6.4 0.2 fusion.30
  6.5 0.5 copy-done.4
  7.0 0.2 copy.21
  7.2 0.2 copy-done.5
  7.5 0.2 copy.22
  7.7 1.5 %copy_bitcast_fusion.1 = (bf16[256,2048]{1,0:T(8,128)(2,1)}, bf16[256,2048]{1,0:T(8,128)(2,1)S(1)}) fusion(bf16[32,8,16,128]{3,2,1,0:T(8,128)(2,1)S(1)} %bitcast.65, bf16[32,8,16,128]{3,2,1,0:T(8,128)(2,1)S(1)} %bitcast.64), kind=kLoop, calls=%fused_computation.29 | loop fusion | bytes 4194304 | tf_op jit(solution)/shard_map/reshape | solution.py:443
  9.2 43.8 %shard_map.119 = (bf16[256,2048]{1,0:T(8,128)(2,1)S(1)}, f32[256,2048]{1,0:T(8,128)}, f32[864,32]{1,0:T(8,128)S(1)}, f32[864,64]{1,0:T(8,128)S(1)}, f32[32,64]{1,0:T(8,128)S(1)}) custom-call(bf16[256,2048]{1,0:T(8,128)(2,1)S(1)} %get-tuple-element.22.rows_ref, bf16[256,2048]{1,0:T(8,128)(2,1)} %get-tuple-element.21.cotangent_ref, ...), custom_call_target="tpu_custom_call" | custom-call | tf_op jit(solution)/shard_map/pallas_call | solution.py:515
  53.0 0.2 copy.38
  53.3 1.3 %copy_bitcast_fusion.3 = bf16[32,8,16,128]{3,2,1,0:T(8,128)(2,1)} fusion(bf16[8,32,16,128]{3,2,1,0:T(8,128)(2,1)S(1)} %bitcast.63), kind=kLoop, calls=%fused_computation.31 | loop fusion | bytes 2097152 | tf_op jit(solution)/shard_map/transpose | solution.py:447
  54.5 0.2 copy-done.3
  54.8 0.4 copy.39
  55.1 1.6 %copy_bitcast_fusion = f32[32,8,16,128]{3,2,1,0:T(8,128)} fusion(f32[8,32,16,128]{3,2,1,0:T(8,128)S(1)} %bitcast.62), kind=kLoop, calls=%fused_computation.8 | loop fusion | bytes 4194304 | tf_op jit(solution)/shard_map/transpose | solution.py:447
  56.7 0.8 %copy.47 = f32[32,32,3,3,3]{1,0,4,3,2:T(8,128)} copy(f32[32,32,3,3,3]{1,0,4,3,2:T(8,128)S(1)} %bitcast.61) | data formatting | bytes 221184
  57.5 0.8 %copy.48 = f32[64,32,3,3,3]{0,1,4,3,2:T(8,128)} copy(f32[64,32,3,3,3]{0,1,4,3,2:T(8,128)S(1)} %bitcast.60) | data formatting | bytes 442368
  58.2 0.6 %copy.49 = f32[32,64]{1,0:T(8,128)} copy(f32[32,64]{1,0:T(8,128)S(1)} %get-tuple-element.34) | data formatting | bytes 16384
  (21 shorter events, 0.9 us)
Async XLA Ops:
  0.6 5.0 %copy-start.6 = (bf16[32,32,3,3,3]{1,0,4,3,2:T(8,128)(2,1)S(1)}, bf16[32,32,3,3,3]{1,0,4,3,2:T(8,128)(2,1)}, u32[]{:S(2)}) copy-start(bf16[32,32,3,3,3]{1,0,4,3,2:T(8,128)(2,1)} %param.10) | copy-start | bytes 165892
  5.8 1.2 %copy-start.4 = (bf16[32,8,16,128]{3,2,1,0:T(8,128)(2,1)S(1)}, bf16[32,8,16,128]{3,2,1,0:T(8,128)(2,1)}, u32[]{:S(2)}) copy-start(bf16[32,8,16,128]{3,2,1,0:T(8,128)(2,1)} %param.8) | copy-start | bytes 3145732
  6.1 1.3 %copy-start.5 = (bf16[32,8,16,128]{3,2,1,0:T(8,128)(2,1)S(1)}, bf16[32,8,16,128]{3,2,1,0:T(8,128)(2,1)}, u32[]{:S(2)}) copy-start(bf16[32,8,16,128]{3,2,1,0:T(8,128)(2,1)} %param.13) | copy-start | bytes 3145732
  7.6 1.5 %copy-start = (bf16[128,512]{1,0:T(8,128)(2,1)S(1)}, bf16[128,512]{1,0:T(8,128)(2,1)}, u32[]{:S(2)}) copy-start(bf16[128,512]{1,0:T(8,128)(2,1)} %constant.8.clone.spread_ref) | copy-start | bytes 393220
  7.7 1.5 %copy-start.1 = (bf16[512,128]{1,0:T(8,128)(2,1)S(1)}, bf16[512,128]{1,0:T(8,128)(2,1)}, u32[]{:S(2)}) copy-start(bf16[512,128]{1,0:T(8,128)(2,1)} %constant.7.clone.pool_ref) | copy-start | bytes 393220
  7.7 1.5 %copy-start.2 = (bf16[32,64]{1,0:T(8,128)(2,1)S(1)}, bf16[32,64]{1,0:T(8,128)(2,1)}, u32[]{:S(2)}) copy-start(bf16[32,64]{1,0:T(8,128)(2,1)} %up_ref.1) | copy-start | bytes 12292
  53.0 1.8 %copy-start.3 = (f32[256,2048]{1,0:T(8,128)S(1)}, f32[256,2048]{1,0:T(8,128)}, u32[]{:S(2)}) copy-start(f32[256,2048]{1,0:T(8,128)} %get-tuple-element.11) | copy-start | bytes 6291460

commit v4 on v3

--- a/solution.py
+++ b/solution.py
@@ -120,6 +120,10 @@
 
 def sigmoid(value):
     return 1.0 / (1.0 + jnp.exp(-value))
+
+
+def near_count(count):
+    return 4 if count % 4 == 0 else 1
 
 
 def whole_step(
@@ -153,60 +157,90 @@
 
     lax.fori_loop(1, count, greet, 0)
 
-    def scatter(refs, d):
-        packed, slots, _, _, send, recv, _, _ = refs
-        chunk = slots.shape[1]
+    fan = near_count(count)
+    outer = count // fan
+    spot, group_of = me % fan, me // fan
+
+    def near(d):
+        return group_of * fan + lax.rem(spot + d, fan)
+
+    def far(d):
+        return lax.rem(me + d * fan, count)
+
+    def rows_of(index, size):
+        return pl.ds(pl.multiple_of(index * size, size), size)
+
+    def remote(source, target, send, recv, device):
         return pltpu.make_async_remote_copy(
-            src_ref=packed.at[pl.ds(pl.multiple_of(peer(d) * chunk, chunk), chunk)],
-            dst_ref=slots.at[d],
-            send_sem=send.at[d],
-            recv_sem=recv.at[d],
-            device_id={"gx": peer(d)},
+            src_ref=source,
+            dst_ref=target,
+            send_sem=send,
+            recv_sem=recv,
+            device_id={"gx": device},
             device_id_type=MESH,
         )
 
-    def collect(refs, d):
-        _, _, part, whole, _, _, send, recv = refs
-        chunk = part.shape[0]
-        return pltpu.make_async_remote_copy(
-            src_ref=part,
-            dst_ref=whole.at[pl.ds(pl.multiple_of(me * chunk, chunk), chunk)],
-            send_sem=send.at[d],
-            recv_sem=recv.at[d],
-            device_id={"gx": peer(d)},
-            device_id_type=MESH,
-        )
-
-    def start(copy, refs):
-        def body(d, carry):
-            copy(refs, d).start()
+    def stage_copy(refs, stage, d):
+        packed, near_slots, near_part, far_slots, far_part, near_whole, whole = refs[:7]
+        send, recv = refs[7 + 2 * stage].at[d], refs[8 + 2 * stage].at[d]
+        block, chunk = near_part.shape[0], far_part.shape[0]
+        if stage == 0:
+            source = packed.at[rows_of(near(d) % fan, block)]
+            return remote(source, near_slots.at[d], send, recv, near(d))
+        if stage == 1:
+            source = near_part.at[rows_of(far(d) // fan, chunk)]
+            return remote(source, far_slots.at[d], send, recv, far(d))
+        if stage == 2:
+            target = near_whole.at[rows_of(group_of, chunk)]
+            return remote(far_part, target, send, recv, far(d))
+        return remote(near_whole, whole.at[rows_of(spot, block)], send, recv, near(d))
+
+    def each(stage, body, init):
+        return lax.fori_loop(1, outer if stage in (1, 2) else fan, body, init)
+
+    def start_stage(refs, stage):
+        packed, near_slots, near_part, far_slots, far_part, near_whole, whole = refs[:7]
+        block, chunk = near_part.shape[0], far_part.shape[0]
+
+        def added(slots):
+            def body(d, total):
+                stage_copy(refs, stage - 1, d).wait_recv()
+                return total + slots[d].astype(F32)
+
+            return body
+
+        def received(d, carry):
+            stage_copy(refs, stage - 1, d).wait_recv()
             return carry
 
-        lax.fori_loop(1, count, body, 0)
-
-    def add_up(refs):
-        packed, slots, part, whole = refs[:4]
-        chunk = part.shape[0]
-        mine = pl.ds(pl.multiple_of(me * chunk, chunk), chunk)
-
-        def add(d, total):
-            scatter(refs, d).wait_recv()
-            return total + slots[d].astype(F32)
-
-        total = lax.fori_loop(1, count, add, packed[mine, :].astype(F32))
-        part[...] = (total * factor).astype(BF16)
-        start(collect, refs)
-        whole[mine, :] = part[...]
+        def begin(d, carry):
+            stage_copy(refs, stage, d).start()
+            return carry
+
+        if stage == 1:
+            first = packed[rows_of(spot, block), :].astype(F32)
+            near_part[...] = each(0, added(near_slots), first).astype(BF16)
+        if stage == 2:
+            first = near_part[rows_of(group_of, chunk), :].astype(F32)
+            far_part[...] = (each(1, added(far_slots), first) * factor).astype(BF16)
+        if stage == 3:
+            near_whole[rows_of(group_of, chunk), :] = far_part[...]
+            each(2, received, 0)
+        each(stage, begin, 0)
 
     def finish(refs):
-        def body(d, carry):
-            scatter(refs, d).wait_send()
-            collect(refs, d).wait_send()
-            collect(refs, d).wait_recv()
-            return carry
-
-        lax.fori_loop(1, count, body, 0)
-        return refs[3][...].astype(F32)
+        near_part, near_whole, whole = refs[2], refs[5], refs[6]
+        whole[rows_of(spot, near_part.shape[0]), :] = near_whole[...]
+        for stage in range(4):
+
+            def body(d, carry, stage=stage):
+                stage_copy(refs, stage, d).wait_send()
+                if stage == 3:
+                    stage_copy(refs, stage, d).wait_recv()
+                return carry
+
+            each(stage, body, 0)
+        return whole[...].astype(F32)
 
     def upward(index, values_ref, edge_ref):
         size = edge_ref.shape[1]
@@ -349,10 +383,11 @@
         ],
         axis=0,
     ).astype(BF16)
-    start(scatter, inner_sum)
+    start_stage(inner_sum, 0)
 
     finish_edges(2, grad_inner_ref, inner_edge)
     gather_edges(gather_coarse, inner_edge, half_y, inner_cols, True)
+    start_stage(inner_sum, 1)
     high, low = halves(dot(coarse_back_ref[...], inner_cols[...]) * 0.125)
     for step in range(steps):
         lanes = slice(step * wide, (step + 1) * wide)
@@ -364,7 +399,7 @@
     start_upward(3, grad_pre_ref, grad_edge)
 
     gather_inner(gather_fine, grad_pre_ref, chans, size_y, fine_cols, True)
-    add_up(inner_sum)
+    start_stage(inner_sum, 2)
 
     def taps_of(plane):
         return dot_nt(
@@ -377,6 +412,7 @@
         grad_fine += taps_of(plane)
     finish_edges(3, grad_pre_ref, grad_edge)
     gather_edges(gather_fine, grad_edge, size_y, fine_cols, True)
+    start_stage(inner_sum, 3)
     grad_fine += taps_of(0) + taps_of(planes + 1)
     tall = 3 * depth // 4
     short = depth - tall
@@ -392,20 +428,16 @@
         axis=0,
     ).astype(BF16)
 
-    def features_grad(group):
+    start_stage(fine_sum, 0)
+    work = [(group, step) for group in range(planes // ALONG) for step in range(steps)]
+    for index, (group, step) in enumerate(work):
         rows = slice(group * ALONG * depth, (group * ALONG + ALONG + 2) * depth)
         held = slice(group * ALONG * chans, (group + 1) * ALONG * chans)
-        for step in range(steps):
-            lanes = slice(step * wide, (step + 1) * wide)
-            grad_rows_ref[held, lanes] = dot(fine_back_ref[...], fine_cols[rows, lanes])
-
-    start(scatter, fine_sum)
-    groups = planes // ALONG
-    for group in range(groups // 2):
-        features_grad(group)
-    add_up(fine_sum)
-    for group in range(groups // 2, groups):
-        features_grad(group)
+        lanes = slice(step * wide, (step + 1) * wide)
+        grad_rows_ref[held, lanes] = dot(fine_back_ref[...], fine_cols[rows, lanes])
+        for stage in (1, 2, 3):
+            if index == stage * len(work) // 4 - 1:
+                start_stage(fine_sum, stage)
     sums = finish(inner_sum)
     grad_coarse_ref[:split, :] = sums[:split, :inner]
     grad_coarse_ref[split:, :] = sums[:split, inner : 2 * inner]
@@ -464,12 +496,18 @@
 
     def sum_scratch(rows, lanes):
         chunk = -(-rows // (16 * count)) * 16
+        fan = near_count(count)
+        outer = count // fan
+        near, far = pltpu.SemaphoreType.DMA((fan,)), pltpu.SemaphoreType.DMA((outer,))
         return (
             pltpu.VMEM((count * chunk, lanes), BF16),
-            pltpu.VMEM((count, chunk, lanes), BF16),
+            pltpu.VMEM((fan, outer * chunk, lanes), BF16),
+            pltpu.VMEM((outer * chunk, lanes), BF16),
+            pltpu.VMEM((outer, chunk, lanes), BF16),
             pltpu.VMEM((chunk, lanes), BF16),
+            pltpu.VMEM((outer * chunk, lanes), BF16),
             pltpu.VMEM((count * chunk, lanes), BF16),
-        ) + (pltpu.SemaphoreType.DMA((count,)),) * 4
+        ) + (near, near, far, far, far, far, near, near)
 
     shape = jax.ShapeDtypeStruct
     args = (

time: 59.2 us -> 64.8 us (1.095)
  Pallas kernels: 43.8 us -> 49.4 us
    pallas_call x1, Pallas kernels: 43.8 us -> 49.4 us  [per_device(): pl.pallas_call(functools.partial(whole_step, count, factor, size_y), out_...]
where the time goes in v4:
time: 64.8 us; the launch traced here: 64.4 us
  Pallas kernels  49.4 us (76%)
  local copies, waits for them, and re-layouts  12.9 us (20%)
  other arithmetic  1.32 us (2%)
  between operations  0.83 us (1%)
    pallas_call x1, Pallas kernels, per_device(): pl.pallas_call(functools.partial(whole_step, count, factor, size_y), out_...  49.4 us
    unnamed x22, local copies, waits for them, and re-layouts  3.99 us
    transpose x2, local copies, waits for them, and re-layouts, channels_first(): return values.reshape(-1, chans, size_z, size_y).transpose(1, 0, 2, 3)  2.83 us
    reshape x1, local copies, waits for them, and re-layouts, planes_first(): return values.transpose(1, 0, 2, 3).reshape(size_x * chans, size_z * size_y)  1.48 us

profile of v4, /device:TPU:0, one launch (start us, length us, event | category | flops | bytes accessed | tf_op | source)
XLA Modules:
  0.0 64.4 jit_solution(14956478802120473088)
XLA Ops:
  0.6 0.7 %convert_bitcast_fusion = f32[2,16]{1,0:T(2,128)S(1)} fusion(s32[1,2,16]{2,1,0:T(2,128)} %param.9), kind=kLoop, calls=%fused_computation.60 | loop fusion | flops 32 | bytes 256 | tf_op jit(solution)/shard_map/broadcast_in_dim | solution.py:485
  1.5 1.1 %copy.24 = bf16[64,864]{1,0:T(8,128)(2,1)S(1)} copy(bf16[64,864]{0,1:T(8,128)(2,1)} %bitcast.71) | data formatting | bytes 221184 | tf_op jit(solution)/shard_map/reshape | solution.py:464
  2.8 1.0 %fusion.34 = (bf16[32,1,288]{0,2,1:T(8,128)(2,1)S(1)}, bf16[32,1,288]{0,2,1:T(8,128)(2,1)S(1)}, bf16[32,1,288]{0,2,1:T(8,128)(2,1)S(1)}) fusion(bf16[32,3,288]{0,2,1:T(8,128)(2,1)} %bitcast.69), kind=kLoop, calls=%fused_computation.61 | loop fusion | bytes 110592 | tf_op jit(solution)/shard_map/slice | solution.py:470
  4.2 1.1 %copy.28 = bf16[32,3,3,3,64]{4,3,2,0,1:T(4,128)(2,1)S(1)} copy(bf16[32,3,3,3,64]{4,0,3,2,1:T(8,128)(2,1)} %bitcast.72) | data formatting | bytes 221184 | tf_op jit(solution)/shard_map/transpose | solution.py:469
  5.3 0.2 reshape.53
  5.6 0.2 copy.23
  5.8 0.2 reshape.51
  6.0 0.1 fusion.22.coarse_back_ref
  6.2 0.2 fusion.13.coarse_taps_ref
  6.4 0.2 fusion.30
  6.5 0.5 copy-done.4
  7.0 0.2 copy.21
  7.2 0.2 copy-done.5
  7.5 0.2 copy.22
  7.7 1.5 %copy_bitcast_fusion.1 = (bf16[256,2048]{1,0:T(8,128)(2,1)}, bf16[256,2048]{1,0:T(8,128)(2,1)S(1)}) fusion(bf16[32,8,16,128]{3,2,1,0:T(8,128)(2,1)S(1)} %bitcast.65, bf16[32,8,16,128]{3,2,1,0:T(8,128)(2,1)S(1)} %bitcast.64), kind=kLoop, calls=%fused_computation.29 | loop fusion | bytes 4194304 | tf_op jit(solution)/shard_map/reshape | solution.py:475
  9.2 49.4 %shard_map.119 = (bf16[256,2048]{1,0:T(8,128)(2,1)S(1)}, f32[256,2048]{1,0:T(8,128)}, f32[864,32]{1,0:T(8,128)S(1)}, f32[864,64]{1,0:T(8,128)S(1)}, f32[32,64]{1,0:T(8,128)S(1)}) custom-call(bf16[256,2048]{1,0:T(8,128)(2,1)S(1)} %get-tuple-element.22.rows_ref, bf16[256,2048]{1,0:T(8,128)(2,1)} %get-tuple-element.21.cotangent_ref, ...), custom_call_target="tpu_custom_call" | custom-call | tf_op jit(solution)/shard_map/pallas_call | solution.py:553
  58.6 0.2 copy.38
  58.8 1.3 %copy_bitcast_fusion.3 = bf16[32,8,16,128]{3,2,1,0:T(8,128)(2,1)} fusion(bf16[8,32,16,128]{3,2,1,0:T(8,128)(2,1)S(1)} %bitcast.63), kind=kLoop, calls=%fused_computation.31 | loop fusion | bytes 2097152 | tf_op jit(solution)/shard_map/transpose | solution.py:479
  60.1 0.2 copy-done.3
  60.4 0.4 copy.39
  60.7 1.6 %copy_bitcast_fusion = f32[32,8,16,128]{3,2,1,0:T(8,128)} fusion(f32[8,32,16,128]{3,2,1,0:T(8,128)S(1)} %bitcast.62), kind=kLoop, calls=%fused_computation.8 | loop fusion | bytes 4194304 | tf_op jit(solution)/shard_map/transpose | solution.py:479
  62.3 0.8 %copy.47 = f32[32,32,3,3,3]{1,0,4,3,2:T(8,128)} copy(f32[32,32,3,3,3]{1,0,4,3,2:T(8,128)S(1)} %bitcast.61) | data formatting | bytes 221184
  63.1 0.8 %copy.48 = f32[64,32,3,3,3]{0,1,4,3,2:T(8,128)} copy(f32[64,32,3,3,3]{0,1,4,3,2:T(8,128)S(1)} %bitcast.60) | data formatting | bytes 442368
  63.8 0.6 copy.49
  (21 shorter events, 0.9 us)
Async XLA Ops:
  0.6 5.0 %copy-start.6 = (bf16[32,32,3,3,3]{1,0,4,3,2:T(8,128)(2,1)S(1)}, bf16[32,32,3,3,3]{1,0,4,3,2:T(8,128)(2,1)}, u32[]{:S(2)}) copy-start(bf16[32,32,3,3,3]{1,0,4,3,2:T(8,128)(2,1)} %param.10) | copy-start | bytes 165892
  5.8 1.2 %copy-start.4 = (bf16[32,8,16,128]{3,2,1,0:T(8,128)(2,1)S(1)}, bf16[32,8,16,128]{3,2,1,0:T(8,128)(2,1)}, u32[]{:S(2)}) copy-start(bf16[32,8,16,128]{3,2,1,0:T(8,128)(2,1)} %param.8) | copy-start | bytes 3145732
  6.1 1.3 %copy-start.5 = (bf16[32,8,16,128]{3,2,1,0:T(8,128)(2,1)S(1)}, bf16[32,8,16,128]{3,2,1,0:T(8,128)(2,1)}, u32[]{:S(2)}) copy-start(bf16[32,8,16,128]{3,2,1,0:T(8,128)(2,1)} %param.13) | copy-start | bytes 3145732
  7.6 1.5 %copy-start = (bf16[128,512]{1,0:T(8,128)(2,1)S(1)}, bf16[128,512]{1,0:T(8,128)(2,1)}, u32[]{:S(2)}) copy-start(bf16[128,512]{1,0:T(8,128)(2,1)} %constant.8.clone.spread_ref) | copy-start | bytes 393220
  7.7 1.5 %copy-start.1 = (bf16[512,128]{1,0:T(8,128)(2,1)S(1)}, bf16[512,128]{1,0:T(8,128)(2,1)}, u32[]{:S(2)}) copy-start(bf16[512,128]{1,0:T(8,128)(2,1)} %constant.7.clone.pool_ref) | copy-start | bytes 393220
  7.7 1.5 %copy-start.2 = (bf16[32,64]{1,0:T(8,128)(2,1)S(1)}, bf16[32,64]{1,0:T(8,128)(2,1)}, u32[]{:S(2)}) copy-start(bf16[32,64]{1,0:T(8,128)(2,1)} %up_ref.1) | copy-start | bytes 12292
  58.6 1.8 %copy-start.3 = (f32[256,2048]{1,0:T(8,128)S(1)}, f32[256,2048]{1,0:T(8,128)}, u32[]{:S(2)}) copy-start(f32[256,2048]{1,0:T(8,128)} %get-tuple-element.11) | copy-start | bytes 6291460
